TPU v7x, 256 devices: a whole 4x4x8 slice. The times are simulated.
256 devices in a mesh: interp: 16 (over z_lo, y), bte: 16 (over z_hi, x, core).
Axes of the slice: x: 4, y: 4, z: 8 (z_hi: 2, z_lo: 4; z = z_hi * 4 + z_lo), core: 2. Of those that a mesh axis runs over, the one named last changes fastest.
Arguments:
- coupling: bfloat16 [2, 64, 120, 4608], P(None, 'interp', None, 'bte'), may hold values from -0.009765625 to 0.009765625
- rvectors: int32 [64, 3], replicated, may hold values from -2 to 2
- qpoints: int32 [2048, 3], P('interp'), may hold values from 0 to 159
- polarization: bfloat16 [2048, 2, 120, 120], P('interp'), may hold values from -0.5 to 0.5
- frequencies: float32 [2048, 120], P('interp'), may hold values from 0.1 to 1
- kbatch: int32 [32], P('bte'), may hold values from 0 to 511
- kq_owner: int32 [65536, 1], P(('interp', 'bte')), may hold values from 0 to 15; in each aligned block of 256 rows (0 to 255, 256 to 511, ...) at most 64 rows name the same one
- kq_row: int32 [65536], P(('interp', 'bte')), may hold values from 0 to 511
- energy: float32 [8192, 12], P('bte'), may hold values from -4 to 4
- band_mask: int32 [8192, 12], P('bte'), may hold values 0 or 1
- deviation: float32 [8192, 3, 12], P('bte'), may hold values from -4.4 to 4.4
- velocity: float32 [32, 3, 12], P('bte'), may hold values from -5 to 5
- impurity: float32 [32, 12], P('bte'), may hold values from 0.2 to 2
Outputs:
- updated_deviation: float32 [32, 3, 12], P('bte')
Inputs may be any that keep to these rules, and one draw needn't show every extreme that they name: `kq_owner`: in the [2, 128] pairs of one device, no owner is named more than 64 times, a bound that some block reaches.
All inputs are finite; a program needn't handle non-finite values. No bound on the sum of `band_mask` on one device may be relied on, other than what follows from the above.
Results may differ from a plain program's by a relative error of at most 0.00091.
Values may be sent and summed in bfloat16 or wider, within the bound.
No kernel may reach another device: no remote copies, remote signals or barrier semaphores. Data moves between devices by JAX's collectives and lax.ppermute only.
A program may use at most 192 MiB of HBM per device.

v0:
```python
import functools

import jax
import jax.numpy as jnp
from jax import lax
from jax.experimental import pallas as pl
from jax.experimental.pallas import tpu as pltpu
from jax.sharding import PartitionSpec as P

GRID = 160
SMEARING = 0.5
THERMAL = 0.3
LOG2_E = 1.4426950408889634
SCALE = (LOG2_E / (2.0 * SMEARING**2)) ** 0.5

BF16 = jnp.bfloat16
F32 = jnp.float32
LANES = 128
SUB = 8
VMEM_LIMIT = 58 * 1024 * 1024

NZ, NY, NX = 4, 4, 4
N_INTERP = NZ * NY

M_HALF, N_THIRD = 6, 3
GROUPS = 2 * M_HALF * N_THIRD
PARTS = ((0, 12), (12, 24))

Q_BLOCK = 16
COL_STRIDE = 264
D_STRIDE = 136
D_BLOCK = 30
UNROLL = 16
PHASE_UNROLL = 3


def params():
    return pltpu.CompilerParams(vmem_limit_bytes=VMEM_LIMIT)


def whole(memory_space=pltpu.VMEM):
    return pl.BlockSpec(memory_space=memory_space)


def cost(flops, bytes_accessed, transcendentals=0):
    return pl.CostEstimate(
        flops=int(flops), bytes_accessed=int(bytes_accessed), transcendentals=int(transcendentals)
    )


def prepare_kernel(kbatch_ref, x_ref, energy_ref, mask_ref, dev_ref, owner_ref, row_ref, *refs):
    outs, (table, ids, near, rows) = refs[:-4], refs[-4:]
    planes, columns, nd = x_ref.shape
    bands, rows_own = energy_ref.shape
    stride = columns + SUB
    for j in range(planes):
        rows[pl.ds(j * stride, columns), 0:nd] = x_ref[j].astype(F32)
    keep = lax.broadcasted_iota(jnp.int32, (2 * SUB, LANES), 1) < nd
    for out, (first, count) in zip(outs, PARTS):
        for g in range(count):
            k, rest = divmod(first + g, M_HALF * N_THIRD)
            m_half, n_third = divmod(rest, N_THIRD)
            for pair in range(4):
                m = 2 * m_half + pair // 2
                n = 4 * n_third + 2 * (pair % 2)
                old = k * 144 + m * 12 + n
                one = rows[pl.ds(old, SUB, stride=stride), :]
                two = rows[pl.ds(old + 1, SUB, stride=stride), :]
                both = jnp.where(keep, jnp.concatenate([one, two], axis=0), 0.0)
                out[4 * g + pair] = both.astype(BF16)
    energies = energy_ref[...]
    mask = mask_ref[...].astype(F32)
    table[0:bands, :] = energies
    for c in range(3):
        table[(c + 1) * bands : (c + 2) * bands, :] = dev_ref[c] * mask
    ids[...] = owner_ref[...] * rows_own + row_ref[...]
    lane = lax.broadcasted_iota(jnp.int32, (bands, rows_own), 1)
    for k in range(2):
        line = jnp.sum(jnp.where(lane == kbatch_ref[k], energies, 0.0), axis=1, keepdims=True)
        line = jnp.broadcast_to(line * SCALE, (bands, LANES))
        for n_third in range(N_THIRD):
            some = line[4 * n_third : 4 * n_third + 4]
            first = (k * N_THIRD + n_third) * SUB
            near[first : first + SUB, :] = jnp.concatenate([some, some], axis=0)


def prepare(kbatch, planes, energy, mask, dev, owner, row):
    n, columns, _ = planes.shape
    bands, rows_own = energy.shape
    return pl.pallas_call(
        prepare_kernel,
        out_shape=[jax.ShapeDtypeStruct((4 * c, 16, LANES), BF16) for _, c in PARTS]
        + [
            jax.ShapeDtypeStruct((4 * bands, rows_own), F32),
            jax.ShapeDtypeStruct(owner.shape, jnp.int32),
            jax.ShapeDtypeStruct((2 * N_THIRD * SUB, LANES), F32),
        ],
        in_specs=[whole(pltpu.SMEM)] + [whole()] * 6,
        out_specs=[whole()] * (len(PARTS) + 3),
        scratch_shapes=[pltpu.VMEM((n * (columns + SUB), LANES), F32)],
        compiler_params=params(),
        cost_estimate=cost(1e5, 1e5),
        name="prepare",
    )(kbatch, planes, energy, mask, dev, owner, row)


def tables_kernel(n_q_total, q_ref, vec_ref, freq_ref, out, freq_out):
    n_q = q_ref.shape[1]
    own = lax.axis_index("interp")
    z, y = own // NY, own % NY
    points = [
        jnp.transpose(jnp.broadcast_to(q_ref[c : c + 1, :].astype(F32), (LANES, n_q)))
        for c in range(3)
    ]
    points = [jnp.concatenate([p, p], axis=1) for p in points]
    vectors = vec_ref[...].astype(F32).astype(BF16)
    lane = lax.broadcasted_iota(jnp.int32, (1, 2 * LANES), 1)
    block, parity, part, vector = lane // 16, lane // 8 % 2, lane // 4 % 2, lane % 4
    number = lax.broadcasted_iota(jnp.int32, (vec_ref.shape[1], 2 * LANES), 0)
    dz, turn = block % 4, block // 4
    dy = jnp.where(turn == 2, 3, jnp.where(turn == 3, 2, turn))
    source = (z - dz + NZ) % NZ * NY + (y - dy + NY) % NY
    pick = jnp.where(number == source * 4 + vector, 1.0, 0.0).astype(BF16)
    chosen = jnp.dot(vectors, pick, preferred_element_type=F32)
    product = sum(points[c] * chosen[c : c + 1, :] for c in range(3))
    product = product + (part * (GRID // 4)).astype(F32)
    for row, turned in enumerate((product, product - GRID // 4)):
        turned = turned - GRID * jnp.floor((turned + 0.5) * (1.0 / GRID))
        value = jnp.cos((2.0 * jnp.pi / GRID) * turned)
        for side in range(2):
            first = (2 * side + row) * n_q
            out[first : first + n_q, :] = jnp.where(parity == side, value, 0.0).astype(BF16)
    modes = freq_ref.shape[0]
    w = jnp.concatenate([freq_ref[...], jnp.ones((LANES - modes, n_q), F32)], axis=0)
    w = jnp.transpose(w)
    occupy = 1.0 / (jnp.exp(w / THERMAL) - 1.0)
    share = 1.0 / (w * n_q_total)
    freq_out[0:n_q, :] = w * SCALE
    freq_out[n_q : 2 * n_q, :] = jnp.log(occupy * share) * LOG2_E
    freq_out[2 * n_q : 3 * n_q, :] = jnp.log((occupy + 1.0) * share) * LOG2_E


def tables(n_q_total, points, vectors, freq):
    n_q = points.shape[1]
    return pl.pallas_call(
        functools.partial(tables_kernel, n_q_total),
        out_shape=[
            jax.ShapeDtypeStruct((4 * n_q, 2 * LANES), BF16),
            jax.ShapeDtypeStruct((3 * n_q, LANES), F32),
        ],
        in_specs=[whole()] * 3,
        out_specs=[whole()] * 2,
        compiler_params=params(),
        cost_estimate=cost(1e5, 1e5),
        name="tables",
    )(points, vectors, freq)


def modes_kernel(nd, nu, turn_steps, pol_ref, out_ref, rows):
    step = pl.program_id(0)

    @pl.when(step < turn_steps)
    def _():
        pad = jnp.zeros((LANES - nu, LANES), F32)

        def one(t, carry):
            plane = jnp.concatenate([pol_ref[t].astype(F32), pad], axis=0)
            first = pl.multiple_of((step * D_BLOCK + t) * D_STRIDE, SUB)
            rows[pl.ds(first, LANES), :] = jnp.transpose(plane)
            return carry

        lax.fori_loop(0, D_BLOCK, one, 0, unroll=10)

    @pl.when(step >= turn_steps)
    def _():
        pad = jnp.zeros((LANES - nd, LANES), F32)

        def one_q(i, carry):
            q = (step - turn_steps) * Q_BLOCK + i
            real = rows[pl.ds(q, nd, stride=D_STRIDE), :]
            imag = rows[pl.ds(nd * D_STRIDE + q, nd, stride=D_STRIDE), :]
            out_ref[i, :, 0:LANES] = jnp.concatenate([real, pad], axis=0).astype(BF16)
            out_ref[i, :, LANES:] = jnp.concatenate([imag, pad], axis=0).astype(BF16)
            return carry

        lax.fori_loop(0, Q_BLOCK, one_q, 0, unroll=4)


def modes(pol):
    planes, nu, n_q = pol.shape
    nd = planes // 2
    turn_steps = planes // D_BLOCK
    return pl.pallas_call(
        functools.partial(modes_kernel, nd, nu, turn_steps),
        grid=(turn_steps + n_q // Q_BLOCK,),
        out_shape=jax.ShapeDtypeStruct((n_q, LANES, 2 * LANES), BF16),
        in_specs=[
            pl.BlockSpec((D_BLOCK, nu, n_q), lambda s: (jnp.minimum(s, turn_steps - 1), 0, 0))
        ],
        out_specs=pl.BlockSpec(
            (Q_BLOCK, LANES, 2 * LANES), lambda s: (jnp.maximum(s - turn_steps, 0), 0, 0)
        ),
        scratch_shapes=[pltpu.VMEM((planes * D_STRIDE, LANES), F32)],
        compiler_params=params(),
        cost_estimate=cost(1e5, 1e5),
        name="modes",
    )(pol)


def lookup_kernel(ids_ref, *refs):
    out = refs[-1]
    n_rows = refs[0].shape[-1]
    me = lax.axis_index("bte")
    half, x, core = me // (2 * NX), me // 2 % NX, me % 2
    ids = ids_ref[...]
    wanted = ids.shape[1]
    row = lax.broadcasted_iota(jnp.int32, (n_rows, wanted), 0)
    total = None
    for ref, dx in zip(refs[:-1], (0, 1, -1, 2)):
        for dc in range(2):
            owner = (half * NX + (x - dx + NX) % NX) * 2 + (core + dc) % 2
            table = ref[dc]
            high = table.astype(BF16)
            rest = table - high.astype(F32)
            middle = rest.astype(BF16)
            low = (rest - middle.astype(F32)).astype(BF16)
            pick = jnp.where(row == ids - owner * n_rows, 1.0, 0.0).astype(BF16)
            got = jnp.dot(
                jnp.concatenate([high, middle, low], axis=0), pick, preferred_element_type=F32
            )
            total = got if total is None else total + got
    n = refs[0].shape[1]
    found = (total[2 * n :] + total[n : 2 * n]) + total[:n]
    out[0] = found[:, : wanted // 2]
    out[1] = found[:, wanted // 2 :]


def lookup(ids, tables):
    n = tables[0].shape[1]
    return pl.pallas_call(
        lookup_kernel,
        out_shape=jax.ShapeDtypeStruct((2, n, ids.shape[1] // 2), F32),
        in_specs=[whole()] * (1 + len(tables)),
        out_specs=whole(),
        compiler_params=params(),
        cost_estimate=cost(1e5, 1e5),
        name="lookup",
    )(ids, *tables)


def totals(got, parts, shape):
    upper = lax.broadcasted_iota(jnp.int32, (SUB, LANES), 0) < 4
    sums = {}
    g = 0
    for part in parts:
        for at in range(part.shape[0] // SUB):
            k, rest = divmod(g, M_HALF * N_THIRD)
            m_half, n_third = divmod(rest, N_THIRD)
            kernel = part[at * SUB : (at + 1) * SUB, :]
            for j in range(4):
                term = kernel
                if j:
                    line = j * 12 + 2 * m_half
                    lanes = slice(k * LANES, (k + 1) * LANES)
                    term = kernel * jnp.where(
                        upper,
                        jnp.broadcast_to(got[line : line + 1, lanes], (SUB, LANES)),
                        jnp.broadcast_to(got[line + 1 : line + 2, lanes], (SUB, LANES)),
                    )
                key = (j, k, n_third)
                sums[key] = sums[key] + term if key in sums else term
            g += 1
    stacked = jnp.concatenate([sums[key] for key in sorted(sums)], axis=0)
    pad = jnp.zeros((shape[1] - stacked.shape[0], LANES), F32)
    return lax.dot_general(
        jnp.ones((shape[0], LANES), F32),
        jnp.concatenate([stacked, pad], axis=0),
        (((1,), (1,)), ((), ())),
        preferred_element_type=F32,
        precision=lax.Precision.HIGHEST,
    )


def columns_kernel(first_group, n_blocks, n_q, earlier, *refs):
    phase_ref, blocks, refs = refs[0], refs[1 : 1 + n_blocks], refs[1 + n_blocks :]
    mode_ref, near_ref, mine_ref, theirs_ref, freq_ref = refs[:5]
    if earlier is None:
        out_ref, field, far_rows = refs[5:]
    else:
        others, (total_ref, field, far_rows, out_ref) = refs[5 : 5 + earlier], refs[5 + earlier :]
    columns = out_ref.shape[0]
    step = pl.program_id(0)

    @pl.when(step == 0)
    def _():
        def two_pairs(p, carry):
            sides = []
            for side in range(2):
                sides.append(
                    jnp.concatenate(
                        [b[:, 2 * p + side].reshape(b.shape[0] * 16, LANES) for b in blocks], axis=0
                    )
                )
            both = jnp.concatenate(sides, axis=1)
            for parity in range(2):
                got = jnp.dot(
                    phase_ref[2 * n_q * parity : 2 * n_q * (parity + 1), :],
                    both,
                    preferred_element_type=F32,
                )
                for side in range(2):
                    column = 4 * p + 2 * side + parity
                    field[pl.ds(pl.multiple_of(column * COL_STRIDE, SUB), 2 * n_q), :] = got[
                        :, side * LANES : (side + 1) * LANES
                    ]
            return carry

        lax.fori_loop(0, columns // 4, two_pairs, 0, unroll=PHASE_UNROLL)
        far = (mine_ref[0, 0:16, :] + theirs_ref[0, 0:16, :]) * SCALE
        for unit in range(columns // (N_THIRD * SUB)):
            k, m_half = divmod(first_group // N_THIRD + unit, M_HALF)
            for side in range(2):
                m = 2 * m_half + side
                line = far[m : m + 1, k * LANES : (k + 1) * LANES]
                turned = jnp.transpose(jnp.broadcast_to(line, (LANES, LANES)))
                for j in range(4):
                    row = unit * SUB + side * 4 + j
                    far_rows[pl.ds(row * D_STRIDE, LANES), :] = turned

    lane = lax.broadcasted_iota(jnp.int32, (columns, LANES), 1)
    units = columns // (N_THIRD * SUB)
    nears = []
    for unit in range(units):
        k = (first_group // N_THIRD + unit) // M_HALF
        nears.append(near_ref[k * N_THIRD * SUB : (k + 1) * N_THIRD * SUB, :])
    near = jnp.concatenate(nears, axis=0).reshape(units, N_THIRD, SUB, LANES)

    def some_q(i, carry):
        rotated = []
        for j in range(UNROLL):
            q = step * Q_BLOCK + i * UNROLL + j
            real = field[pl.ds(q, columns, stride=COL_STRIDE), :].astype(BF16)
            imag = field[pl.ds(q + n_q, columns, stride=COL_STRIDE), :].astype(BF16)
            mode = mode_ref[i * UNROLL + j]
            turn = jnp.concatenate([-mode[:, LANES:], mode[:, :LANES]], axis=1)
            rotated.append(
                jnp.dot(
                    jnp.concatenate([real, imag], axis=1),
                    jnp.concatenate([mode, turn], axis=0),
                    preferred_element_type=F32,
                )
            )
        out = out_ref[...]
        for j in range(UNROLL):
            q = step * Q_BLOCK + i * UNROLL + j
            far = far_rows[pl.ds(q, units * SUB, stride=D_STRIDE), :]
            gap = (near - far.reshape(units, 1, SUB, LANES)).reshape(columns, LANES)
            w = freq_ref[pl.ds(q, 1), :]
            plus, minus = gap + w, gap - w
            weight = jnp.exp2(freq_ref[pl.ds(n_q + q, 1), :] - plus * plus) + jnp.exp2(
                freq_ref[pl.ds(2 * n_q + q, 1), :] - minus * minus
            )
            real, imag = rotated[j][:, :LANES], rotated[j][:, LANES:]
            terms = (real * real + imag * imag) * weight
            out = jnp.where(lane == q, jnp.sum(terms, axis=1, keepdims=True), out)
        out_ref[...] = out
        return carry

    lax.fori_loop(0, Q_BLOCK // UNROLL, some_q, 0)

    if earlier is not None:

        @pl.when(step == pl.num_programs(0) - 1)
        def _():
            got = totals(mine_ref[0] + theirs_ref[0], [*others, out_ref], total_ref.shape[1:])
            for i in range(total_ref.shape[0]):
                total_ref[i] = got


def columns_of(index, phase, blocks, mode, near, mine, theirs, freq, others=None):
    n_q = mode.shape[0]
    first, groups = PARTS[index]
    columns = SUB * groups
    fixed = lambda shape: pl.BlockSpec(shape, lambda s: (0,) * len(shape))
    operands = [phase, *blocks]
    rest = [near, mine, theirs, freq, *(others or [])]
    sums = (columns, LANES)
    out = sums if others is None else (N_INTERP, SUB, 2 * LANES)
    return pl.pallas_call(
        functools.partial(
            columns_kernel, first, len(blocks), n_q, None if others is None else len(others)
        ),
        grid=(n_q // Q_BLOCK,),
        out_shape=jax.ShapeDtypeStruct(out, F32),
        in_specs=[fixed(o.shape) for o in operands]
        + [pl.BlockSpec((Q_BLOCK, LANES, 2 * LANES), lambda s: (s, 0, 0))]
        + [fixed(o.shape) for o in rest],
        out_specs=fixed(out),
        scratch_shapes=[
            pltpu.VMEM((columns * COL_STRIDE, LANES), F32),
            pltpu.VMEM((columns // N_THIRD * D_STRIDE, LANES), F32),
        ]
        + ([] if others is None else [pltpu.VMEM(sums, F32)]),
        compiler_params=params(),
        cost_estimate=cost(1e5, 1e5),
        name="columns",
    )(*operands, mode, *rest)


def interp_pairs(dz, dy):
    return [
        (z * NY + y, (z + dz) % NZ * NY + (y + dy) % NY) for z in range(NZ) for y in range(NY)
    ]


def bte_pairs(dh, dx, dc):
    return [
        ((h * NX + x) * 2 + c, ((h + dh) % 2 * NX + (x + dx) % NX) * 2 + (c + dc) % 2)
        for h in range(2)
        for x in range(NX)
        for c in range(2)
    ]


def along_interp(value, dz, dy):
    return lax.ppermute(value, "interp", interp_pairs(dz, dy))


def along_bte(value, dh, dx, dc):
    return lax.ppermute(value, "bte", bte_pairs(dh, dx, dc))


def after(value, *others):
    return lax.optimization_barrier((value, *others))[0]


def both_ways(own):
    return along_interp(own, 0, 1), along_interp(own, 0, -1)


def local(
    coupling,
    rvectors,
    qpoints,
    polarization,
    frequencies,
    kbatch,
    kq_owner,
    kq_row,
    energy,
    band_mask,
    deviation,
    velocity,
    impurity,
):
    n_q = qpoints.shape[0]
    nbands = energy.shape[1]
    nmodes = frequencies.shape[1]
    q_total = n_q * lax.axis_size("interp")
    columns = coupling.shape[3]

    planes = jnp.swapaxes(coupling, 2, 3).reshape(-1, columns, nmodes)
    *own_parts, own_table, ids, near = prepare(
        kbatch,
        planes,
        energy.T,
        band_mask.T,
        jnp.transpose(deviation, (1, 2, 0)),
        kq_owner.reshape(1, -1),
        kq_row.reshape(1, -1),
    )
    own_first, own_second = own_parts

    other_ids = along_bte(ids, 1, 0, 0)
    phase, freq = tables(q_total, *after((qpoints.T, rvectors.T, frequencies.T), ids))
    other_table = along_bte(own_table, 0, 0, 1)

    def behind(own, *before):
        one, three = along_interp(own, 1, 0), along_interp(own, -1, 0)
        two = along_interp(after(one, *before), 1, 0)
        return jnp.stack([own, one]), jnp.stack([two, three])

    chip_table = jnp.stack([own_table, other_table])
    near_tables = [along_bte(chip_table, 0, dx, 0) for dx in (1, -1, 2)]

    first_near, first_late = behind(own_first, freq, other_ids)
    first_up, first_down = both_ways(first_near)
    late_up, late_down = both_ways(first_late)
    first_far = along_interp(first_up, 0, 1), along_interp(late_down, 0, -1)
    first = (first_near, first_late, first_up, late_up, first_down, late_down, *first_far)

    second_near, second_late = behind(
        after(own_second, first_late, other_ids), late_up, late_down, first_up, first_down, *near_tables
    )
    second_up, second_down = both_ways(after(second_near, first_up, late_down))
    second_late_up, second_late_down = both_ways(after(second_late, *first_far))

    pol = jnp.transpose(polarization, (1, 2, 3, 0)).reshape(2 * nmodes, nmodes, n_q)
    mode = modes(after(pol, second_late, *first_far))

    all_ids = jnp.concatenate([ids, other_ids], axis=1)
    found = lookup(after(all_ids, mode), [chip_table] + near_tables)
    mine, theirs = found, along_bte(found[1:], 1, 0, 0)

    second_far = (
        along_interp(after(second_up, *first_far, found), 0, 1),
        along_interp(after(second_late_down, *first_far, found), 0, -1),
    )
    second = (
        second_near,
        second_late,
        second_up,
        second_late_up,
        second_down,
        second_late_down,
        *second_far,
    )

    rest = (mode, near, mine, theirs, freq)
    sums = columns_of(0, phase, first, *rest)
    total = columns_of(1, phase, second, *rest, others=[sums])
    near_mask = band_mask[kbatch].astype(F32)

    total = lax.all_to_all(total, "interp", 0, 0, tiled=True)[:, 0].sum(axis=0)
    total = total[: 4 * 48].reshape(4, 2, N_THIRD, 2, 4).sum(axis=3).reshape(4, 2, nbands)
    scatter_rate = total[0]
    inflow = jnp.transpose(total[1:], (1, 0, 2))
    return near_mask[:, None, :] * (velocity + inflow) / (scatter_rate + impurity)[:, None, :]


def solution(mesh):
    in_specs = (
        P(None, "interp", None, "bte"),
        P(),
        P("interp", None),
        P("interp", None, None, None),
        P("interp", None),
        P("bte"),
        P(("interp", "bte"), None),
        P(("interp", "bte")),
        P("bte", None),
        P("bte", None),
        P("bte", None, None),
        P("bte", None, None),
        P("bte", None),
    )
    out_specs = P("bte", None, None)
    return jax.shard_map(local, mesh=mesh, in_specs=in_specs, out_specs=out_specs, check_vma=False)
```

profile of v0, /device:TPU:6, one launch (start us, length us, event | category | flops | bytes accessed | tf_op | source)
XLA Modules:
  0.0 148.7 jit_solution(14156189466190424948)
XLA Ops:
  0.0 2.3 %prepare.1 = (bf16[48,16,128]{2,1,0:T(8,128)(2,1)}, bf16[96,16,128]{2,1,0:T(8,128)(2,1)}, f32[48,512]{1,0:T(8,128)}, s32[1,256]{1,0:T(1,128)}, f32[48,128]{1,0:T(8,128)}) custom-call(s32[2]{0:T(128)} %kbatch_ref.1, bf16[8,288,120]{2,1,0:T(8,128)(2,1)} %bitcast.32, f32[12,512]{1,0:T(8,128)} %bitcast.46, s32[12,512]{1,0:T(8,128)} %bitcast.41, ...), custom_call_target="tpu_custom_call" | custom-call | flops 100000 | bytes 100000 | tf_op jit(solution)/shard_map/prepare/pallas_call | solution.py:90
  2.3 1.9 %collective-permute-start = (bf16[48,16,128]{2,1,0:T(8,128)(2,1)}, bf16[48,16,128]{2,1,0:T(8,128)(2,1)S(1)}, u32[]{:S(2)}, u32[]{:S(2)}) collective-permute-start(bf16[48,16,128]{2,1,0:T(8,128)(2,1)} %get-tuple-element.30), channel_id=1, source_target_pairs={{0,64},{16,80},{32,96},{48,112},{64,128},{80,144},{96,160},{112,17... | collective-permute-start | bytes 589832 | tf_op jit(solution)/shard_map/ppermute | solution.py:426
  4.2 6.3 %collective-permute-start.1 = (s32[1,256]{1,0:T(1,128)}, s32[1,256]{1,0:T(1,128)S(1)}, u32[]{:S(2)}, u32[]{:S(2)}) collective-permute-start(s32[1,256]{1,0:T(1,128)} %get-tuple-element.24), channel_id=1, source_target_pairs={{0,8},{1,9},{2,10},{3,11},{4,12},{5,13},{6,14},{7,15},{8,0},{9,1},... | collective-permute-start | bytes 3080 | tf_op jit(solution)/shard_map/ppermute | solution.py:430
  10.5 2.8 %collective-permute-start.3 = (bf16[48,16,128]{2,1,0:T(8,128)(2,1)}, bf16[48,16,128]{2,1,0:T(8,128)(2,1)S(1)}, u32[]{:S(2)}, u32[]{:S(2)}) collective-permute-start(bf16[48,16,128]{2,1,0:T(8,128)(2,1)} %get-tuple-element.30), channel_id=1, source_target_pairs={{0,192},{16,208},{32,224},{48,240},{64,0},{80,16},{96,32},{112,48}... | collective-permute-start | bytes 589832 | tf_op jit(solution)/shard_map/ppermute | solution.py:426
  13.3 2.8 %tables.1 = (bf16[512,256]{1,0:T(8,128)(2,1)}, f32[384,128]{1,0:T(8,128)}) custom-call(s32[3,128]{1,0:T(4,128)} %bitcast.48, s32[3,64]{1,0:T(4,128)} %bitcast.49, f32[120,128]{1,0:T(8,128)} %bitcast.45), custom_call_target="tpu_custom_call" | custom-call | flops 100000 | bytes 100000 | tf_op jit(solution)/shard_map/tables/pallas_call | solution.py:145
  16.2 0.9 pad_maximum_fusion.4.refs_0_
  17.1 0.6 collective-permute-start.10
  17.6 1.5 %collective-permute-start.11 = (f32[2,48,512]{2,1,0:T(8,128)S(1)}, f32[2,48,512]{2,1,0:T(8,128)}, u32[]{:S(2)}, u32[]{:S(2)}) collective-permute-start(f32[2,48,512]{2,1,0:T(8,128)S(1)} %pad_maximum_fusion.4.refs_0_), channel_id=1, source_target_pairs={{0,6},{1,7},{2,0},{3,1},{4,2},{5,3},{6,4},{7,5},{8,14},{9,15},{10,... | collective-permute-start | bytes 589832 | tf_op jit(solution)/shard_map/ppermute | solution.py:430
  19.2 1.4 collective-permute-start.12
  20.6 1.0 pad_maximum_fusion.3.refs_1_
  21.6 1.7 %collective-permute-start.7 = (bf16[2,48,16,128]{3,2,1,0:T(8,128)(2,1)S(1)}, bf16[2,48,16,128]{3,2,1,0:T(8,128)(2,1)S(1)}, u32[]{:S(2)}, u32[]{:S(2)}) collective-permute-start(bf16[2,48,16,128]{3,2,1,0:T(8,128)(2,1)S(1)} %pad_maximum_fusion.3.refs_1_), channel_id=1, source_target_pairs={{0,16},{16,32},{32,48},{48,0},{64,80},{80,96},{96,112},{112,64},{1... | collective-permute-start | bytes 1179656 | tf_op jit(solution)/shard_map/ppermute | solution.py:426
  23.2 1.5 collective-permute-done.2
  24.7 3.0 %collective-permute-start.8 = (bf16[2,48,16,128]{3,2,1,0:T(8,128)(2,1)S(1)}, bf16[2,48,16,128]{3,2,1,0:T(8,128)(2,1)S(1)}, u32[]{:S(2)}, u32[]{:S(2)}) collective-permute-start(bf16[2,48,16,128]{3,2,1,0:T(8,128)(2,1)S(1)} %pad_maximum_fusion.3.refs_1_), channel_id=1, source_target_pairs={{0,48},{16,0},{32,16},{48,32},{64,112},{80,64},{96,80},{112,96},{1... | collective-permute-start | bytes 1179656 | tf_op jit(solution)/shard_map/ppermute | solution.py:426
  27.8 0.8 collective-permute-start.6
  28.6 1.0 collective-permute-done.11.refs_2_
  29.7 1.7 %collective-permute-start.5 = (bf16[2,48,16,128]{3,2,1,0:T(8,128)(2,1)S(1)}, bf16[2,48,16,128]{3,2,1,0:T(8,128)(2,1)S(1)}, u32[]{:S(2)}, u32[]{:S(2)}) collective-permute-start(bf16[2,48,16,128]{3,2,1,0:T(8,128)(2,1)S(1)} %pad_maximum_fusion.2.refs_2_), channel_id=1, source_target_pairs={{0,16},{16,32},{32,48},{48,0},{64,80},{80,96},{96,112},{112,64},{1... | collective-permute-start | bytes 1179656 | tf_op jit(solution)/shard_map/ppermute | solution.py:426
  31.3 2.8 %collective-permute-done.7.refs_3_ = bf16[2,48,16,128]{3,2,1,0:T(8,128)(2,1)S(1)} collective-permute-done((bf16[2,48,16,128]{3,2,1,0:T(8,128)(2,1)S(1)}, bf16[2,48,16,128]{3,2,1,0:T(8,128)(2,1)S(1)}, u32[]{:S(2)}, u32[]{:S(2)}) %collective-permute-start.7) | collective-permute-done | bytes 393248 | tf_op jit(solution)/shard_map/ppermute | solution.py:426
  34.1 3.9 %collective-permute-start.14 = (bf16[96,16,128]{2,1,0:T(8,128)(2,1)}, bf16[96,16,128]{2,1,0:T(8,128)(2,1)S(1)}, u32[]{:S(2)}, u32[]{:S(2)}) collective-permute-start(bf16[96,16,128]{2,1,0:T(8,128)(2,1)} %get-tuple-element.33), channel_id=1, source_target_pairs={{0,192},{16,208},{32,224},{48,240},{64,0},{80,16},{96,32},{112,48}... | collective-permute-start | bytes 1179656 | tf_op jit(solution)/shard_map/ppermute | solution.py:426
  38.0 5.8 %collective-permute-done.4 = bf16[96,16,128]{2,1,0:T(8,128)(2,1)S(1)} collective-permute-done((bf16[96,16,128]{2,1,0:T(8,128)(2,1)}, bf16[96,16,128]{2,1,0:T(8,128)(2,1)S(1)}, u32[]{:S(2)}, u32[]{:S(2)}) %collective-permute-start.4) | collective-permute-done | bytes 393248 | tf_op jit(solution)/shard_map/ppermute | solution.py:426
  43.8 2.1 %collective-permute-start.13 = (bf16[96,16,128]{2,1,0:T(8,128)(2,1)S(1)}, bf16[96,16,128]{2,1,0:T(8,128)(2,1)S(1)}, u32[]{:S(2)}, u32[]{:S(2)}) collective-permute-start(bf16[96,16,128]{2,1,0:T(8,128)(2,1)S(1)} %collective-permute-done.4), channel_id=1, source_target_pairs={{0,64},{16,80},{32,96},{48,112},{64,128},{80,144},{96,160},{112,17... | collective-permute-start | bytes 1179656 | tf_op jit(solution)/shard_map/ppermute | solution.py:426
  45.9 1.3 collective-permute-start.16
  47.1 2.0 %collective-permute-start.17 = (bf16[2,48,16,128]{3,2,1,0:T(8,128)(2,1)S(1)}, bf16[2,48,16,128]{3,2,1,0:T(8,128)(2,1)S(1)}, u32[]{:S(2)}, u32[]{:S(2)}) collective-permute-start(bf16[2,48,16,128]{3,2,1,0:T(8,128)(2,1)S(1)} %collective-permute-done.6.refs_6_), channel_id=1, source_target_pairs={{0,48},{16,0},{32,16},{48,32},{64,112},{80,64},{96,80},{112,96},{1... | collective-permute-start | bytes 1179656 | tf_op jit(solution)/shard_map/ppermute | solution.py:426
  49.1 1.1 pad_maximum_fusion.refs_1_
  50.2 0.2 collective-permute-start.15
  50.3 0.7 collective-permute-done.14
  51.1 6.2 %collective-permute-done.13 = bf16[96,16,128]{2,1,0:T(8,128)(2,1)S(1)} collective-permute-done((bf16[96,16,128]{2,1,0:T(8,128)(2,1)S(1)}, bf16[96,16,128]{2,1,0:T(8,128)(2,1)S(1)}, u32[]{:S(2)}, u32[]{:S(2)}) %collective-permute-start.13) | collective-permute-done | bytes 393248 | tf_op jit(solution)/shard_map/ppermute | solution.py:426
  57.4 1.7 %collective-permute-done.16.refs_7_ = bf16[2,48,16,128]{3,2,1,0:T(8,128)(2,1)S(1)} collective-permute-done((bf16[2,48,16,128]{3,2,1,0:T(8,128)(2,1)S(1)}, bf16[2,48,16,128]{3,2,1,0:T(8,128)(2,1)S(1)}, u32[]{:S(2)}, u32[]{:S(2)}) %collective-permute-start.16) | collective-permute-done | bytes 393248 | tf_op jit(solution)/shard_map/ppermute | solution.py:426
  59.1 1.3 collective-permute-start.20
  60.4 1.2 pad_add_fusion.ids_ref
  61.6 0.7 collective-permute-start.19
  62.3 1.3 collective-permute-start.18
  63.7 14.0 %modes.1.refs_9_ = bf16[128,128,256]{2,1,0:T(8,128)(2,1)} custom-call(bf16[240,120,128]{2,1,0:T(8,128)(2,1)} %bitcast.31), custom_call_target="tpu_custom_call" | custom-call | flops 100000 | bytes 100000 | tf_op jit(solution)/shard_map/modes/pallas_call | solution.py:193
  77.7 2.8 %lookup.1.refs_11_ = f32[2,48,256]{2,1,0:T(8,128)} custom-call(s32[1,512]{1,0:T(1,128)} %pad_add_fusion.ids_ref, f32[2,48,512]{2,1,0:T(8,128)} %copy-done.6, f32[2,48,512]{2,1,0:T(8,128)} %copy-done.13, f32[2,48,512]{2,1,0:T(8,128)} %collective-permute-done.11.refs_2_, f32[2,48,512]{2,1,0:T(8,128)} %copy-done.14), custom_call_target="tpu_custom_call" | custom-call | flops 100000 | bytes 100000 | tf_op jit(solution)/shard_map/lookup/pallas_call | solution.py:240
  80.5 0.9 collective-permute-start.21
  81.4 2.4 %collective-permute-start.22 = (bf16[2,96,16,128]{3,2,1,0:T(8,128)(2,1)}, bf16[2,96,16,128]{3,2,1,0:T(8,128)(2,1)}, u32[]{:S(2)}, u32[]{:S(2)}) collective-permute-start(bf16[2,96,16,128]{3,2,1,0:T(8,128)(2,1)} %collective-permute-done.20.refs_6_), channel_id=1, source_target_pairs={{0,48},{16,0},{32,16},{48,32},{64,112},{80,64},{96,80},{112,96},{1... | collective-permute-start | bytes 2359304 | tf_op jit(solution)/shard_map/ppermute | solution.py:426
  83.8 0.8 slice.27
  84.6 0.2 collective-permute-start.23
  84.9 0.1 copy.18
  85.0 7.6 %collective-permute-done.23.refs_12_ = f32[1,48,256]{2,1,0:T(8,128)S(1)} collective-permute-done((f32[1,48,256]{2,1,0:T(8,128)S(1)}, f32[1,48,256]{2,1,0:T(8,128)S(1)}, u32[]{:S(2)}, u32[]{:S(2)}) %collective-permute-start.23) | collective-permute-done | bytes 49184 | tf_op jit(solution)/shard_map/ppermute | solution.py:430
  92.6 0.6 copy-done.15
  93.2 14.3 %columns.2.refs_14_ = f32[96,128]{1,0:T(8,128)} custom-call(bf16[512,256]{1,0:T(8,128)(2,1)} %get-tuple-element.28.refs_0_, bf16[2,48,16,128]{3,2,1,0:T(8,128)(2,1)} %copy-done.2, bf16[2,48,16,128]{3,2,1,0:T(8,128)(2,1)} %copy-done.3, bf16[2,48,16,128]{3,2,1,0:T(8,128)(2,1)} %copy-done.7, bf16[2,48,16,128]{3,2,1,0:T(8,128)(2,1)} %copy-done.10, ...), custom_call_target="tpu_custom_call" | custom-call | flops 100000 | bytes 100000 | tf_op jit(solution)/shard_map/columns/pallas_call | solution.py:389
  107.6 1.1 collective-permute-done.22.refs_8_
  108.7 21.0 %columns.3 = f32[16,8,256]{2,1,0:T(8,128)} custom-call(bf16[512,256]{1,0:T(8,128)(2,1)} %get-tuple-element.28.refs_0_, bf16[2,96,16,128]{3,2,1,0:T(8,128)(2,1)} %copy-done, bf16[2,96,16,128]{3,2,1,0:T(8,128)(2,1)} %copy-done.1, bf16[2,96,16,128]{3,2,1,0:T(8,128)(2,1)} %copy-done.4, bf16[2,96,16,128]{3,2,1,0:T(8,128)(2,1)} %collective-permute-done.18.refs_4_, ...), custom_call_target="tpu_custom_call" | custom-call | flops 100000 | bytes 100000 | tf_op jit(solution)/shard_map/columns/pallas_call | solution.py:389
  129.7 9.1 %all-to-all-start = ((f32[16,8,256]{2,1,0:T(8,128)}), f32[16,8,256]{2,1,0:T(8,128)S(1)}, u32[]{:S(2)}, u32[]{:S(2)}) async-start(f32[16,8,256]{2,1,0:T(8,128)} %columns.3), calls=%async_computation | async-start | bytes 262144 | tf_op jit(solution)/shard_map/all_to_all | solution.py:524
  138.8 0.6 gather_fusion
  139.4 8.3 %all-to-all-done = f32[16,8,256]{2,1,0:T(8,128)S(1)} async-done(((f32[16,8,256]{2,1,0:T(8,128)}), f32[16,8,256]{2,1,0:T(8,128)S(1)}, u32[]{:S(2)}, u32[]{:S(2)}) %all-to-all-start) | async-done | bytes 131104 | tf_op jit(solution)/shard_map/all_to_all | solution.py:524
  147.7 0.1 reshape.27
  148.1 0.6 fusion.1
  (69 shorter events, 0.6 us)
Async XLA Ops:
  2.3 13.8 %collective-permute-start = (bf16[48,16,128]{2,1,0:T(8,128)(2,1)}, bf16[48,16,128]{2,1,0:T(8,128)(2,1)S(1)}, u32[]{:S(2)}, u32[]{:S(2)}) collective-permute-start(bf16[48,16,128]{2,1,0:T(8,128)(2,1)} %get-tuple-element.30), channel_id=1, source_target_pairs={{0,64},{16,80},{32,96},{48,112},{64,128},{80,144},{96,160},{112,17... | collective-permute-start | bytes 589832 | tf_op jit(solution)/shard_map/ppermute | solution.py:426
  4.2 12.0 %collective-permute-start.9 = (f32[48,512]{1,0:T(8,128)}, f32[48,512]{1,0:T(8,128)S(1)}, u32[]{:S(2)}, u32[]{:S(2)}) collective-permute-start(f32[48,512]{1,0:T(8,128)} %get-tuple-element.34), channel_id=1, source_target_pairs={{0,1},{1,0},{2,3},{3,2},{4,5},{5,4},{6,7},{7,6},{8,9},{9,8},{10,11... | collective-permute-start | bytes 294920 | tf_op jit(solution)/shard_map/ppermute | solution.py:430
  4.2 11.9 %collective-permute-start.1 = (s32[1,256]{1,0:T(1,128)}, s32[1,256]{1,0:T(1,128)S(1)}, u32[]{:S(2)}, u32[]{:S(2)}) collective-permute-start(s32[1,256]{1,0:T(1,128)} %get-tuple-element.24), channel_id=1, source_target_pairs={{0,8},{1,9},{2,10},{3,11},{4,12},{5,13},{6,14},{7,15},{8,0},{9,1},... | collective-permute-start | bytes 3080 | tf_op jit(solution)/shard_map/ppermute | solution.py:430
  10.5 11.1 %collective-permute-start.3 = (bf16[48,16,128]{2,1,0:T(8,128)(2,1)}, bf16[48,16,128]{2,1,0:T(8,128)(2,1)S(1)}, u32[]{:S(2)}, u32[]{:S(2)}) collective-permute-start(bf16[48,16,128]{2,1,0:T(8,128)(2,1)} %get-tuple-element.30), channel_id=1, source_target_pairs={{0,192},{16,208},{32,224},{48,240},{64,0},{80,16},{96,32},{112,48}... | collective-permute-start | bytes 589832 | tf_op jit(solution)/shard_map/ppermute | solution.py:426
  16.1 8.6 %collective-permute-start.2 = (bf16[48,16,128]{2,1,0:T(8,128)(2,1)S(1)}, bf16[48,16,128]{2,1,0:T(8,128)(2,1)S(1)}, u32[]{:S(2)}, u32[]{:S(2)}) collective-permute-start(bf16[48,16,128]{2,1,0:T(8,128)(2,1)S(1)} %collective-permute-done), channel_id=1, source_target_pairs={{0,64},{16,80},{32,96},{48,112},{64,128},{80,144},{96,160},{112,17... | collective-permute-start | bytes 589832 | tf_op jit(solution)/shard_map/ppermute | solution.py:426
  17.1 60.6 %copy-start.6 = (f32[2,48,512]{2,1,0:T(8,128)}, f32[2,48,512]{2,1,0:T(8,128)S(1)}, u32[]{:S(2)}) copy-start(f32[2,48,512]{2,1,0:T(8,128)S(1)} %pad_maximum_fusion.4.refs_0_) | copy-start | bytes 589828
  17.1 10.7 %collective-permute-start.10 = (f32[2,48,512]{2,1,0:T(8,128)S(1)}, f32[2,48,512]{2,1,0:T(8,128)S(1)}, u32[]{:S(2)}, u32[]{:S(2)}) collective-permute-start(f32[2,48,512]{2,1,0:T(8,128)S(1)} %pad_maximum_fusion.4.refs_0_), channel_id=1, source_target_pairs={{0,2},{1,3},{2,4},{3,5},{4,6},{5,7},{6,0},{7,1},{8,10},{9,11},{10,... | collective-permute-start | bytes 589832 | tf_op jit(solution)/shard_map/ppermute | solution.py:430
  17.6 12.0 %collective-permute-start.11 = (f32[2,48,512]{2,1,0:T(8,128)S(1)}, f32[2,48,512]{2,1,0:T(8,128)}, u32[]{:S(2)}, u32[]{:S(2)}) collective-permute-start(f32[2,48,512]{2,1,0:T(8,128)S(1)} %pad_maximum_fusion.4.refs_0_), channel_id=1, source_target_pairs={{0,6},{1,7},{2,0},{3,1},{4,2},{5,3},{6,4},{7,5},{8,14},{9,15},{10,... | collective-permute-start | bytes 589832 | tf_op jit(solution)/shard_map/ppermute | solution.py:430
  19.2 10.5 %collective-permute-start.12 = (f32[2,48,512]{2,1,0:T(8,128)S(1)}, f32[2,48,512]{2,1,0:T(8,128)S(1)}, u32[]{:S(2)}, u32[]{:S(2)}) collective-permute-start(f32[2,48,512]{2,1,0:T(8,128)S(1)} %pad_maximum_fusion.4.refs_0_), channel_id=1, source_target_pairs={{0,4},{1,5},{2,6},{3,7},{4,0},{5,1},{6,2},{7,3},{8,12},{9,13},{10,... | collective-permute-start | bytes 589832 | tf_op jit(solution)/shard_map/ppermute | solution.py:430
  21.6 56.1 %copy-start.2 = (bf16[2,48,16,128]{3,2,1,0:T(8,128)(2,1)}, bf16[2,48,16,128]{3,2,1,0:T(8,128)(2,1)S(1)}, u32[]{:S(2)}) copy-start(bf16[2,48,16,128]{3,2,1,0:T(8,128)(2,1)S(1)} %pad_maximum_fusion.3.refs_1_) | copy-start | bytes 1179652
  21.6 12.5 %collective-permute-start.7 = (bf16[2,48,16,128]{3,2,1,0:T(8,128)(2,1)S(1)}, bf16[2,48,16,128]{3,2,1,0:T(8,128)(2,1)S(1)}, u32[]{:S(2)}, u32[]{:S(2)}) collective-permute-start(bf16[2,48,16,128]{3,2,1,0:T(8,128)(2,1)S(1)} %pad_maximum_fusion.3.refs_1_), channel_id=1, source_target_pairs={{0,16},{16,32},{32,48},{48,0},{64,80},{80,96},{96,112},{112,64},{1... | collective-permute-start | bytes 1179656 | tf_op jit(solution)/shard_map/ppermute | solution.py:426
  24.7 13.3 %collective-permute-start.8 = (bf16[2,48,16,128]{3,2,1,0:T(8,128)(2,1)S(1)}, bf16[2,48,16,128]{3,2,1,0:T(8,128)(2,1)S(1)}, u32[]{:S(2)}, u32[]{:S(2)}) collective-permute-start(bf16[2,48,16,128]{3,2,1,0:T(8,128)(2,1)S(1)} %pad_maximum_fusion.3.refs_1_), channel_id=1, source_target_pairs={{0,48},{16,0},{32,16},{48,32},{64,112},{80,64},{96,80},{112,96},{1... | collective-permute-start | bytes 1179656 | tf_op jit(solution)/shard_map/ppermute | solution.py:426
  27.8 49.9 %copy-start.3 = (bf16[2,48,16,128]{3,2,1,0:T(8,128)(2,1)}, bf16[2,48,16,128]{3,2,1,0:T(8,128)(2,1)S(1)}, u32[]{:S(2)}) copy-start(bf16[2,48,16,128]{3,2,1,0:T(8,128)(2,1)S(1)} %pad_maximum_fusion.2.refs_2_) | copy-start | bytes 1179652
  27.8 0.8 copy-start.13
  27.8 16.0 %collective-permute-start.6 = (bf16[2,48,16,128]{3,2,1,0:T(8,128)(2,1)S(1)}, bf16[2,48,16,128]{3,2,1,0:T(8,128)(2,1)S(1)}, u32[]{:S(2)}, u32[]{:S(2)}) collective-permute-start(bf16[2,48,16,128]{3,2,1,0:T(8,128)(2,1)S(1)} %pad_maximum_fusion.2.refs_2_), channel_id=1, source_target_pairs={{0,48},{16,0},{32,16},{48,32},{64,112},{80,64},{96,80},{112,96},{1... | collective-permute-start | bytes 1179656 | tf_op jit(solution)/shard_map/ppermute | solution.py:426
  29.6 14.1 %collective-permute-start.4 = (bf16[96,16,128]{2,1,0:T(8,128)(2,1)}, bf16[96,16,128]{2,1,0:T(8,128)(2,1)S(1)}, u32[]{:S(2)}, u32[]{:S(2)}) collective-permute-start(bf16[96,16,128]{2,1,0:T(8,128)(2,1)} %get-tuple-element.33), channel_id=1, source_target_pairs={{0,64},{16,80},{32,96},{48,112},{64,128},{80,144},{96,160},{112,17... | collective-permute-start | bytes 1179656 | tf_op jit(solution)/shard_map/ppermute | solution.py:426
  29.7 1.7 %copy-start.14 = (f32[2,48,512]{2,1,0:T(8,128)}, f32[2,48,512]{2,1,0:T(8,128)S(1)}, u32[]{:S(2)}) copy-start(f32[2,48,512]{2,1,0:T(8,128)S(1)} %collective-permute-done.12.refs_3_) | copy-start | bytes 589828
  29.7 14.1 %collective-permute-start.5 = (bf16[2,48,16,128]{3,2,1,0:T(8,128)(2,1)S(1)}, bf16[2,48,16,128]{3,2,1,0:T(8,128)(2,1)S(1)}, u32[]{:S(2)}, u32[]{:S(2)}) collective-permute-start(bf16[2,48,16,128]{3,2,1,0:T(8,128)(2,1)S(1)} %pad_maximum_fusion.2.refs_2_), channel_id=1, source_target_pairs={{0,16},{16,32},{32,48},{48,0},{64,80},{80,96},{96,112},{112,64},{1... | collective-permute-start | bytes 1179656 | tf_op jit(solution)/shard_map/ppermute | solution.py:426
  34.1 43.6 %copy-start.7 = (bf16[2,48,16,128]{3,2,1,0:T(8,128)(2,1)}, bf16[2,48,16,128]{3,2,1,0:T(8,128)(2,1)S(1)}, u32[]{:S(2)}) copy-start(bf16[2,48,16,128]{3,2,1,0:T(8,128)(2,1)S(1)} %collective-permute-done.7.refs_3_) | copy-start | bytes 1179652
  34.1 16.9 %collective-permute-start.14 = (bf16[96,16,128]{2,1,0:T(8,128)(2,1)}, bf16[96,16,128]{2,1,0:T(8,128)(2,1)S(1)}, u32[]{:S(2)}, u32[]{:S(2)}) collective-permute-start(bf16[96,16,128]{2,1,0:T(8,128)(2,1)} %get-tuple-element.33), channel_id=1, source_target_pairs={{0,192},{16,208},{32,224},{48,240},{64,0},{80,16},{96,32},{112,48}... | collective-permute-start | bytes 1179656 | tf_op jit(solution)/shard_map/ppermute | solution.py:426
  38.0 5.8 %copy-start.8 = (bf16[2,48,16,128]{3,2,1,0:T(8,128)(2,1)}, bf16[2,48,16,128]{3,2,1,0:T(8,128)(2,1)S(1)}, u32[]{:S(2)}) copy-start(bf16[2,48,16,128]{3,2,1,0:T(8,128)(2,1)S(1)} %collective-permute-done.8.refs_5_) | copy-start | bytes 1179652
  43.8 33.9 %copy-start.9 = (bf16[2,48,16,128]{3,2,1,0:T(8,128)(2,1)}, bf16[2,48,16,128]{3,2,1,0:T(8,128)(2,1)S(1)}, u32[]{:S(2)}) copy-start(bf16[2,48,16,128]{3,2,1,0:T(8,128)(2,1)S(1)} %collective-permute-done.6.refs_6_) | copy-start | bytes 1179652
  43.8 5.3 %copy-start.10 = (bf16[2,48,16,128]{3,2,1,0:T(8,128)(2,1)}, bf16[2,48,16,128]{3,2,1,0:T(8,128)(2,1)S(1)}, u32[]{:S(2)}) copy-start(bf16[2,48,16,128]{3,2,1,0:T(8,128)(2,1)S(1)} %collective-permute-done.5.refs_4_) | copy-start | bytes 1179652
  43.8 13.5 %collective-permute-start.13 = (bf16[96,16,128]{2,1,0:T(8,128)(2,1)S(1)}, bf16[96,16,128]{2,1,0:T(8,128)(2,1)S(1)}, u32[]{:S(2)}, u32[]{:S(2)}) collective-permute-start(bf16[96,16,128]{2,1,0:T(8,128)(2,1)S(1)} %collective-permute-done.4), channel_id=1, source_target_pairs={{0,64},{16,80},{32,96},{48,112},{64,128},{80,144},{96,160},{112,17... | collective-permute-start | bytes 1179656 | tf_op jit(solution)/shard_map/ppermute | solution.py:426
  45.9 13.3 %collective-permute-start.16 = (bf16[2,48,16,128]{3,2,1,0:T(8,128)(2,1)S(1)}, bf16[2,48,16,128]{3,2,1,0:T(8,128)(2,1)S(1)}, u32[]{:S(2)}, u32[]{:S(2)}) collective-permute-start(bf16[2,48,16,128]{3,2,1,0:T(8,128)(2,1)S(1)} %collective-permute-done.7.refs_3_), channel_id=1, source_target_pairs={{0,16},{16,32},{32,48},{48,0},{64,80},{80,96},{96,112},{112,64},{1... | collective-permute-start | bytes 1179656 | tf_op jit(solution)/shard_map/ppermute | solution.py:426
  47.1 12.0 %collective-permute-start.17 = (bf16[2,48,16,128]{3,2,1,0:T(8,128)(2,1)S(1)}, bf16[2,48,16,128]{3,2,1,0:T(8,128)(2,1)S(1)}, u32[]{:S(2)}, u32[]{:S(2)}) collective-permute-start(bf16[2,48,16,128]{3,2,1,0:T(8,128)(2,1)S(1)} %collective-permute-done.6.refs_6_), channel_id=1, source_target_pairs={{0,48},{16,0},{32,16},{48,32},{64,112},{80,64},{96,80},{112,96},{1... | collective-permute-start | bytes 1179656 | tf_op jit(solution)/shard_map/ppermute | solution.py:426
  50.2 27.5 %copy-start = (bf16[2,96,16,128]{3,2,1,0:T(8,128)(2,1)}, bf16[2,96,16,128]{3,2,1,0:T(8,128)(2,1)S(1)}, u32[]{:S(2)}) copy-start(bf16[2,96,16,128]{3,2,1,0:T(8,128)(2,1)S(1)} %pad_maximum_fusion.refs_1_) | copy-start | bytes 2359300
  50.2 30.3 %collective-permute-start.15 = (bf16[2,96,16,128]{3,2,1,0:T(8,128)(2,1)S(1)}, bf16[2,96,16,128]{3,2,1,0:T(8,128)(2,1)S(1)}, u32[]{:S(2)}, u32[]{:S(2)}) collective-permute-start(bf16[2,96,16,128]{3,2,1,0:T(8,128)(2,1)S(1)} %pad_maximum_fusion.refs_1_), channel_id=1, source_target_pairs={{0,16},{16,32},{32,48},{48,0},{64,80},{80,96},{96,112},{112,64},{1... | collective-permute-start | bytes 2359304 | tf_op jit(solution)/shard_map/ppermute | solution.py:426
  57.4 27.7 %copy-start.1 = (bf16[2,96,16,128]{3,2,1,0:T(8,128)(2,1)}, bf16[2,96,16,128]{3,2,1,0:T(8,128)(2,1)S(1)}, u32[]{:S(2)}) copy-start(bf16[2,96,16,128]{3,2,1,0:T(8,128)(2,1)S(1)} %pad_maximum_fusion.1.refs_2_) | copy-start | bytes 2359300
  57.4 27.5 %copy-start.16 = (s32[512,12]{0,1:T(8,128)S(1)}, s32[512,12]{0,1:T(8,128)}, u32[]{:S(2)}) copy-start(s32[512,12]{0,1:T(8,128)} %param.22) | copy-start | bytes 73732
  59.1 21.4 %copy-start.11 = (bf16[2,48,16,128]{3,2,1,0:T(8,128)(2,1)}, bf16[2,48,16,128]{3,2,1,0:T(8,128)(2,1)S(1)}, u32[]{:S(2)}) copy-start(bf16[2,48,16,128]{3,2,1,0:T(8,128)(2,1)S(1)} %collective-permute-done.16.refs_7_) | copy-start | bytes 1179652
  59.1 21.4 %copy-start.12 = (bf16[2,48,16,128]{3,2,1,0:T(8,128)(2,1)}, bf16[2,48,16,128]{3,2,1,0:T(8,128)(2,1)S(1)}, u32[]{:S(2)}) copy-start(bf16[2,48,16,128]{3,2,1,0:T(8,128)(2,1)S(1)} %collective-permute-done.17.refs_8_) | copy-start | bytes 1179652
  59.1 22.3 %collective-permute-start.20 = (bf16[2,96,16,128]{3,2,1,0:T(8,128)(2,1)S(1)}, bf16[2,96,16,128]{3,2,1,0:T(8,128)(2,1)}, u32[]{:S(2)}, u32[]{:S(2)}) collective-permute-start(bf16[2,96,16,128]{3,2,1,0:T(8,128)(2,1)S(1)} %pad_maximum_fusion.1.refs_2_), channel_id=1, source_target_pairs={{0,48},{16,0},{32,16},{48,32},{64,112},{80,64},{96,80},{112,96},{1... | collective-permute-start | bytes 2359304 | tf_op jit(solution)/shard_map/ppermute | solution.py:426
  61.6 45.9 %collective-permute-start.19 = (bf16[2,96,16,128]{3,2,1,0:T(8,128)(2,1)S(1)}, bf16[2,96,16,128]{3,2,1,0:T(8,128)(2,1)}, u32[]{:S(2)}, u32[]{:S(2)}) collective-permute-start(bf16[2,96,16,128]{3,2,1,0:T(8,128)(2,1)S(1)} %pad_maximum_fusion.refs_1_), channel_id=1, source_target_pairs={{0,48},{16,0},{32,16},{48,32},{64,112},{80,64},{96,80},{112,96},{1... | collective-permute-start | bytes 2359304 | tf_op jit(solution)/shard_map/ppermute | solution.py:426
  62.3 45.2 %collective-permute-start.18 = (bf16[2,96,16,128]{3,2,1,0:T(8,128)(2,1)S(1)}, bf16[2,96,16,128]{3,2,1,0:T(8,128)(2,1)}, u32[]{:S(2)}, u32[]{:S(2)}) collective-permute-start(bf16[2,96,16,128]{3,2,1,0:T(8,128)(2,1)S(1)} %pad_maximum_fusion.1.refs_2_), channel_id=1, source_target_pairs={{0,16},{16,32},{32,48},{48,0},{64,80},{80,96},{96,112},{112,64},{1... | collective-permute-start | bytes 2359304 | tf_op jit(solution)/shard_map/ppermute | solution.py:426
  80.5 28.2 %copy-start.4 = (bf16[2,96,16,128]{3,2,1,0:T(8,128)(2,1)}, bf16[2,96,16,128]{3,2,1,0:T(8,128)(2,1)S(1)}, u32[]{:S(2)}) copy-start(bf16[2,96,16,128]{3,2,1,0:T(8,128)(2,1)S(1)} %collective-permute-done.15.refs_3_) | copy-start | bytes 2359300
  80.5 27.0 %collective-permute-start.21 = (bf16[2,96,16,128]{3,2,1,0:T(8,128)(2,1)S(1)}, bf16[2,96,16,128]{3,2,1,0:T(8,128)(2,1)S(1)}, u32[]{:S(2)}, u32[]{:S(2)}) collective-permute-start(bf16[2,96,16,128]{3,2,1,0:T(8,128)(2,1)S(1)} %collective-permute-done.15.refs_3_), channel_id=1, source_target_pairs={{0,16},{16,32},{32,48},{48,0},{64,80},{80,96},{96,112},{112,64},{1... | collective-permute-start | bytes 2359304 | tf_op jit(solution)/shard_map/ppermute | solution.py:426
  81.4 27.2 %collective-permute-start.22 = (bf16[2,96,16,128]{3,2,1,0:T(8,128)(2,1)}, bf16[2,96,16,128]{3,2,1,0:T(8,128)(2,1)}, u32[]{:S(2)}, u32[]{:S(2)}) collective-permute-start(bf16[2,96,16,128]{3,2,1,0:T(8,128)(2,1)} %collective-permute-done.20.refs_6_), channel_id=1, source_target_pairs={{0,48},{16,0},{32,16},{48,32},{64,112},{80,64},{96,80},{112,96},{1... | collective-permute-start | bytes 2359304 | tf_op jit(solution)/shard_map/ppermute | solution.py:426
  84.6 8.0 %collective-permute-start.23 = (f32[1,48,256]{2,1,0:T(8,128)S(1)}, f32[1,48,256]{2,1,0:T(8,128)S(1)}, u32[]{:S(2)}, u32[]{:S(2)}) collective-permute-start(f32[1,48,256]{2,1,0:T(8,128)S(1)} %slice.27), channel_id=1, source_target_pairs={{0,8},{1,9},{2,10},{3,11},{4,12},{5,13},{6,14},{7,15},{8,0},{9,1},... | collective-permute-start | bytes 147464 | tf_op jit(solution)/shard_map/ppermute | solution.py:430
  92.6 0.6 copy-start.15
  107.5 31.3 %copy-start.19 = (s32[2]{0:T(128)S(1)}, s32[2]{0:T(128)}, u32[]{:S(2)}) copy-start(s32[2]{0:T(128)} %kbatch_ref.1) | copy-start | bytes 28
  107.5 40.6 %copy-start.18 = (f32[2,12]{1,0:T(2,128)S(1)}, f32[2,12]{1,0:T(2,128)}, u32[]{:S(2)}) copy-start(f32[2,12]{1,0:T(2,128)} %param.25) | copy-start | bytes 292
  107.5 40.6 %copy-start.17 = (f32[2,3,12]{2,0,1:T(2,128)S(1)}, f32[2,3,12]{2,0,1:T(2,128)}, u32[]{:S(2)}) copy-start(f32[2,3,12]{2,0,1:T(2,128)} %param.24) | copy-start | bytes 868
  107.6 1.1 copy-start.5
  129.7 18.0 %all-to-all-start = ((f32[16,8,256]{2,1,0:T(8,128)}), f32[16,8,256]{2,1,0:T(8,128)S(1)}, u32[]{:S(2)}, u32[]{:S(2)}) async-start(f32[16,8,256]{2,1,0:T(8,128)} %columns.3), calls=%async_computation | async-start | bytes 262144 | tf_op jit(solution)/shard_map/all_to_all | solution.py:524
where the time goes:
time: 149 us
  Pallas kernels  57.1 us (38%)
  starting transfers between devices  47 us (32%)
  waiting for transfers between devices  36.8 us (25%)
  other arithmetic  4.98 us (3%)
  local copies, waits for them, and re-layouts  2.48 us (2%)
    pallas_call x2, Pallas kernels, columns_of(): pl.pallas_call(functools.partial(columns_kernel, first, len(blocks), n_q,...  35.3 us
    ppermute x18, starting transfers between devices, along_interp(): return lax.ppermute(value, 'interp', interp_pairs(dz, dy))  27.9 us
    ppermute x18, waiting for transfers between devices, along_interp(): return lax.ppermute(value, 'interp', interp_pairs(dz, dy))  19.9 us
    pallas_call x1, Pallas kernels, modes(): pl.pallas_call(functools.partial(modes_kernel, nd, nu, turn_steps), grid=...  14 us
    ppermute x6, starting transfers between devices, along_bte(): return lax.ppermute(value, 'bte', bte_pairs(dh, dx, dc))  10 us
    all_to_all x1, starting transfers between devices, local(): total = lax.all_to_all(total, 'interp', 0, 0, tiled=True)[:, 0].sum(axis=0)  9.06 us
    ppermute x6, waiting for transfers between devices, along_bte(): return lax.ppermute(value, 'bte', bte_pairs(dh, dx, dc))  8.65 us
    all_to_all x1, waiting for transfers between devices, local(): total = lax.all_to_all(total, 'interp', 0, 0, tiled=True)[:, 0].sum(axis=0)  8.32 us
  transfers between devices with their start and end apart: 25, of which 10 were waited for; matrix products, arithmetic and copies ran while one was open for 4% of the time, Pallas kernels for 23%

commit v1 on v0

--- a/solution.py
+++ b/solution.py
@@ -483,6 +483,10 @@
     chip_table = jnp.stack([own_table, other_table])
     near_tables = [along_bte(chip_table, 0, dx, 0) for dx in (1, -1, 2)]
 
+    all_ids = jnp.concatenate([ids, other_ids], axis=1)
+    found = lookup(all_ids, [chip_table] + near_tables)
+    mine, theirs = found, along_bte(found[1:], 1, 0, 0)
+
     first_near, first_late = behind(own_first, freq, other_ids)
     first_up, first_down = both_ways(first_near)
     late_up, late_down = both_ways(first_late)
@@ -490,7 +494,7 @@
     first = (first_near, first_late, first_up, late_up, first_down, late_down, *first_far)
 
     second_near, second_late = behind(
-        after(own_second, first_late, other_ids), late_up, late_down, first_up, first_down, *near_tables
+        after(own_second, first_late, other_ids), late_up, late_down, first_up, first_down, found
     )
     second_up, second_down = both_ways(after(second_near, first_up, late_down))
     second_late_up, second_late_down = both_ways(after(second_late, *first_far))
@@ -498,13 +502,9 @@
     pol = jnp.transpose(polarization, (1, 2, 3, 0)).reshape(2 * nmodes, nmodes, n_q)
     mode = modes(after(pol, second_late, *first_far))
 
-    all_ids = jnp.concatenate([ids, other_ids], axis=1)
-    found = lookup(after(all_ids, mode), [chip_table] + near_tables)
-    mine, theirs = found, along_bte(found[1:], 1, 0, 0)
-
     second_far = (
-        along_interp(after(second_up, *first_far, found), 0, 1),
-        along_interp(after(second_late_down, *first_far, found), 0, -1),
+        along_interp(after(second_up, mode, theirs), 0, 1),
+        along_interp(after(second_late_down, mode, theirs), 0, -1),
     )
     second = (
         second_near,

time: 149 us -> 147 us (0.987)
  starting transfers between devices: 47 us -> 44.7 us
    ppermute x6, waiting for transfers between devices: 8.65 us -> 0.95 us  [along_bte(): return lax.ppermute(value, 'bte', bte_pairs(dh, dx, dc))]
    ppermute x18, waiting for transfers between devices: 19.9 us -> 27.2 us  [along_interp(): return lax.ppermute(value, 'interp', interp_pairs(dz, dy))]
    all_to_all x1, starting transfers between devices: 9.06 us -> 6.38 us  [local(): total = lax.all_to_all(total, 'interp', 0, 0, tiled=True)[:, 0].sum(axis=0)]
  transfers between devices with their start and end apart: 25 -> 25, of which waited for: 10 -> 11; matrix products, arithmetic and copies ran while one was open for 4% -> 4% of each run, Pallas kernels for 23% -> 23%
where the time goes in v1:
time: 147 us; the launch traced here: 146 us
  Pallas kernels  57.1 us (39%)
  starting transfers between devices  44.7 us (30%)
  waiting for transfers between devices  36.4 us (25%)
  other arithmetic  4.99 us (3%)
  local copies, waits for them, and re-layouts  2.27 us (2%)
    pallas_call x2, Pallas kernels, columns_of(): pl.pallas_call(functools.partial(columns_kernel, first, len(blocks), n_q,...  35.3 us
    ppermute x18, waiting for transfers between devices, along_interp(): return lax.ppermute(value, 'interp', interp_pairs(dz, dy))  27.2 us
    ppermute x18, starting transfers between devices, along_interp(): return lax.ppermute(value, 'interp', interp_pairs(dz, dy))  27 us
    pallas_call x1, Pallas kernels, modes(): pl.pallas_call(functools.partial(modes_kernel, nd, nu, turn_steps), grid=...  14 us
    ppermute x6, starting transfers between devices, along_bte(): return lax.ppermute(value, 'bte', bte_pairs(dh, dx, dc))  11.3 us
    all_to_all x1, waiting for transfers between devices, local(): total = lax.all_to_all(total, 'interp', 0, 0, tiled=True)[:, 0].sum(axis=0)  8.32 us
    all_to_all x1, starting transfers between devices, local(): total = lax.all_to_all(total, 'interp', 0, 0, tiled=True)[:, 0].sum(axis=0)  6.38 us
  transfers between devices with their start and end apart: 25, of which 11 were waited for; matrix products, arithmetic and copies ran while one was open for 4% of the time, Pallas kernels for 23%

profile of v1, /device:TPU:6, one launch (start us, length us, event | category | flops | bytes accessed | tf_op | source)
XLA Modules:
  0.0 145.8 jit_solution(8204998059419597025)
XLA Ops:
  0.0 2.3 %prepare.1 = (bf16[48,16,128]{2,1,0:T(8,128)(2,1)}, bf16[96,16,128]{2,1,0:T(8,128)(2,1)}, f32[48,512]{1,0:T(8,128)}, s32[1,256]{1,0:T(1,128)}, f32[48,128]{1,0:T(8,128)}) custom-call(s32[2]{0:T(128)} %kbatch_ref.1, bf16[8,288,120]{2,1,0:T(8,128)(2,1)} %bitcast.32, f32[12,512]{1,0:T(8,128)} %bitcast.46, s32[12,512]{1,0:T(8,128)} %bitcast.41, ...), custom_call_target="tpu_custom_call" | custom-call | flops 100000 | bytes 100000 | tf_op jit(solution)/shard_map/prepare/pallas_call | solution.py:90
  2.3 1.9 %collective-permute-start = (bf16[48,16,128]{2,1,0:T(8,128)(2,1)}, bf16[48,16,128]{2,1,0:T(8,128)(2,1)S(1)}, u32[]{:S(2)}, u32[]{:S(2)}) collective-permute-start(bf16[48,16,128]{2,1,0:T(8,128)(2,1)} %get-tuple-element.29), channel_id=1, source_target_pairs={{0,64},{16,80},{32,96},{48,112},{64,128},{80,144},{96,160},{112,17... | collective-permute-start | bytes 589832 | tf_op jit(solution)/shard_map/ppermute | solution.py:426
  4.2 6.3 %collective-permute-start.1 = (s32[1,256]{1,0:T(1,128)}, s32[1,256]{1,0:T(1,128)S(1)}, u32[]{:S(2)}, u32[]{:S(2)}) collective-permute-start(s32[1,256]{1,0:T(1,128)} %get-tuple-element.23), channel_id=1, source_target_pairs={{0,8},{1,9},{2,10},{3,11},{4,12},{5,13},{6,14},{7,15},{8,0},{9,1},... | collective-permute-start | bytes 3080 | tf_op jit(solution)/shard_map/ppermute | solution.py:430
  10.5 2.8 %collective-permute-start.3 = (bf16[48,16,128]{2,1,0:T(8,128)(2,1)}, bf16[48,16,128]{2,1,0:T(8,128)(2,1)S(1)}, u32[]{:S(2)}, u32[]{:S(2)}) collective-permute-start(bf16[48,16,128]{2,1,0:T(8,128)(2,1)} %get-tuple-element.29), channel_id=1, source_target_pairs={{0,192},{16,208},{32,224},{48,240},{64,0},{80,16},{96,32},{112,48}... | collective-permute-start | bytes 589832 | tf_op jit(solution)/shard_map/ppermute | solution.py:426
  13.3 2.8 %tables.1 = (bf16[512,256]{1,0:T(8,128)(2,1)}, f32[384,128]{1,0:T(8,128)}) custom-call(s32[3,128]{1,0:T(4,128)} %bitcast.48, s32[3,64]{1,0:T(4,128)} %bitcast.49, f32[120,128]{1,0:T(8,128)} %bitcast.45), custom_call_target="tpu_custom_call" | custom-call | flops 100000 | bytes 100000 | tf_op jit(solution)/shard_map/tables/pallas_call | solution.py:145
  16.1 0.9 pad_maximum_fusion.4.refs_0_
  17.1 0.6 collective-permute-start.10
  17.6 1.5 %collective-permute-start.11 = (f32[2,48,512]{2,1,0:T(8,128)S(1)}, f32[2,48,512]{2,1,0:T(8,128)S(1)}, u32[]{:S(2)}, u32[]{:S(2)}) collective-permute-start(f32[2,48,512]{2,1,0:T(8,128)S(1)} %pad_maximum_fusion.4.refs_0_), channel_id=1, source_target_pairs={{0,6},{1,7},{2,0},{3,1},{4,2},{5,3},{6,4},{7,5},{8,14},{9,15},{10,... | collective-permute-start | bytes 589832 | tf_op jit(solution)/shard_map/ppermute | solution.py:430
  19.2 1.4 collective-permute-start.12
  20.6 1.0 pad_maximum_fusion.3.refs_1_
  21.6 1.7 %collective-permute-start.7 = (bf16[2,48,16,128]{3,2,1,0:T(8,128)(2,1)S(1)}, bf16[2,48,16,128]{3,2,1,0:T(8,128)(2,1)S(1)}, u32[]{:S(2)}, u32[]{:S(2)}) collective-permute-start(bf16[2,48,16,128]{3,2,1,0:T(8,128)(2,1)S(1)} %pad_maximum_fusion.3.refs_1_), channel_id=1, source_target_pairs={{0,16},{16,32},{32,48},{48,0},{64,80},{80,96},{96,112},{112,64},{1... | collective-permute-start | bytes 1179656 | tf_op jit(solution)/shard_map/ppermute | solution.py:426
  23.2 1.5 collective-permute-done.2
  24.7 3.0 %collective-permute-start.8 = (bf16[2,48,16,128]{3,2,1,0:T(8,128)(2,1)S(1)}, bf16[2,48,16,128]{3,2,1,0:T(8,128)(2,1)S(1)}, u32[]{:S(2)}, u32[]{:S(2)}) collective-permute-start(bf16[2,48,16,128]{3,2,1,0:T(8,128)(2,1)S(1)} %pad_maximum_fusion.3.refs_1_), channel_id=1, source_target_pairs={{0,48},{16,0},{32,16},{48,32},{64,112},{80,64},{96,80},{112,96},{1... | collective-permute-start | bytes 1179656 | tf_op jit(solution)/shard_map/ppermute | solution.py:426
  27.8 0.8 collective-permute-start.6
  28.6 0.9 collective-permute-done.11.refs_2_
  29.5 1.7 %collective-permute-start.5 = (bf16[2,48,16,128]{3,2,1,0:T(8,128)(2,1)S(1)}, bf16[2,48,16,128]{3,2,1,0:T(8,128)(2,1)S(1)}, u32[]{:S(2)}, u32[]{:S(2)}) collective-permute-start(bf16[2,48,16,128]{3,2,1,0:T(8,128)(2,1)S(1)} %pad_maximum_fusion.2.refs_2_), channel_id=1, source_target_pairs={{0,16},{16,32},{32,48},{48,0},{64,80},{80,96},{96,112},{112,64},{1... | collective-permute-start | bytes 1179656 | tf_op jit(solution)/shard_map/ppermute | solution.py:426
  31.2 1.2 pad_add_fusion.ids_ref
  32.5 2.8 %lookup.1.refs_11_ = f32[2,48,256]{2,1,0:T(8,128)} custom-call(s32[1,512]{1,0:T(1,128)} %pad_add_fusion.ids_ref, f32[2,48,512]{2,1,0:T(8,128)} %copy-done.6, f32[2,48,512]{2,1,0:T(8,128)} %copy-done.13, f32[2,48,512]{2,1,0:T(8,128)} %copy-done.14, f32[2,48,512]{2,1,0:T(8,128)} %copy-done.15), custom_call_target="tpu_custom_call" | custom-call | flops 100000 | bytes 100000 | tf_op jit(solution)/shard_map/lookup/pallas_call | solution.py:240
  35.2 3.7 %collective-permute-start.14 = (bf16[96,16,128]{2,1,0:T(8,128)(2,1)}, bf16[96,16,128]{2,1,0:T(8,128)(2,1)S(1)}, u32[]{:S(2)}, u32[]{:S(2)}) collective-permute-start(bf16[96,16,128]{2,1,0:T(8,128)(2,1)} %get-tuple-element.32), channel_id=1, source_target_pairs={{0,192},{16,208},{32,224},{48,240},{64,0},{80,16},{96,32},{112,48}... | collective-permute-start | bytes 1179656 | tf_op jit(solution)/shard_map/ppermute | solution.py:426
  39.0 3.6 %collective-permute-done.4 = bf16[96,16,128]{2,1,0:T(8,128)(2,1)S(1)} collective-permute-done((bf16[96,16,128]{2,1,0:T(8,128)(2,1)}, bf16[96,16,128]{2,1,0:T(8,128)(2,1)S(1)}, u32[]{:S(2)}, u32[]{:S(2)}) %collective-permute-start.4) | collective-permute-done | bytes 393248 | tf_op jit(solution)/shard_map/ppermute | solution.py:426
  42.6 1.2 collective-permute-done.6.refs_6_
  43.7 0.5 collective-permute-start.13
  44.3 1.1 collective-permute-start.16
  45.3 2.7 %collective-permute-start.17 = (bf16[2,48,16,128]{3,2,1,0:T(8,128)(2,1)S(1)}, bf16[2,48,16,128]{3,2,1,0:T(8,128)(2,1)S(1)}, u32[]{:S(2)}, u32[]{:S(2)}) collective-permute-start(bf16[2,48,16,128]{3,2,1,0:T(8,128)(2,1)S(1)} %collective-permute-done.6.refs_6_), channel_id=1, source_target_pairs={{0,48},{16,0},{32,16},{48,32},{64,112},{80,64},{96,80},{112,96},{1... | collective-permute-start | bytes 1179656 | tf_op jit(solution)/shard_map/ppermute | solution.py:426
  48.0 1.1 pad_maximum_fusion.refs_1_
  49.1 1.5 %collective-permute-done.14 = bf16[96,16,128]{2,1,0:T(8,128)(2,1)S(1)} collective-permute-done((bf16[96,16,128]{2,1,0:T(8,128)(2,1)}, bf16[96,16,128]{2,1,0:T(8,128)(2,1)S(1)}, u32[]{:S(2)}, u32[]{:S(2)}) %collective-permute-start.14) | collective-permute-done | bytes 393248 | tf_op jit(solution)/shard_map/ppermute | solution.py:426
  50.7 6.3 %collective-permute-done.13 = bf16[96,16,128]{2,1,0:T(8,128)(2,1)S(1)} collective-permute-done((bf16[96,16,128]{2,1,0:T(8,128)(2,1)S(1)}, bf16[96,16,128]{2,1,0:T(8,128)(2,1)S(1)}, u32[]{:S(2)}, u32[]{:S(2)}) %collective-permute-start.13) | collective-permute-done | bytes 393248 | tf_op jit(solution)/shard_map/ppermute | solution.py:426
  57.1 0.9 collective-permute-done.16.refs_7_
  58.0 2.1 %collective-permute-start.20 = (bf16[2,96,16,128]{3,2,1,0:T(8,128)(2,1)S(1)}, bf16[2,96,16,128]{3,2,1,0:T(8,128)(2,1)}, u32[]{:S(2)}, u32[]{:S(2)}) collective-permute-start(bf16[2,96,16,128]{3,2,1,0:T(8,128)(2,1)S(1)} %pad_maximum_fusion.1.refs_2_), channel_id=1, source_target_pairs={{0,48},{16,0},{32,16},{48,32},{64,112},{80,64},{96,80},{112,96},{1... | collective-permute-start | bytes 2359304 | tf_op jit(solution)/shard_map/ppermute | solution.py:426
  60.1 0.8 slice.27
  60.9 1.5 %collective-permute-start.21 = (f32[1,48,256]{2,1,0:T(8,128)S(1)}, f32[1,48,256]{2,1,0:T(8,128)S(1)}, u32[]{:S(2)}, u32[]{:S(2)}) collective-permute-start(f32[1,48,256]{2,1,0:T(8,128)S(1)} %slice.27), channel_id=1, source_target_pairs={{0,8},{1,9},{2,10},{3,11},{4,12},{5,13},{6,14},{7,15},{8,0},{9,1},... | collective-permute-start | bytes 147464 | tf_op jit(solution)/shard_map/ppermute | solution.py:430
  62.4 0.7 collective-permute-start.19
  63.1 1.3 collective-permute-start.18
  64.4 14.0 %modes.1.refs_9_ = bf16[128,128,256]{2,1,0:T(8,128)(2,1)} custom-call(bf16[240,120,128]{2,1,0:T(8,128)(2,1)} %bitcast.31), custom_call_target="tpu_custom_call" | custom-call | flops 100000 | bytes 100000 | tf_op jit(solution)/shard_map/modes/pallas_call | solution.py:193
  78.5 0.1 collective-permute-done.20.refs_6_
  78.6 0.4 copy-done.16
  79.0 2.8 %collective-permute-start.23 = (bf16[2,96,16,128]{3,2,1,0:T(8,128)(2,1)}, bf16[2,96,16,128]{3,2,1,0:T(8,128)(2,1)}, u32[]{:S(2)}, u32[]{:S(2)}) collective-permute-start(bf16[2,96,16,128]{3,2,1,0:T(8,128)(2,1)} %collective-permute-done.20.refs_6_), channel_id=1, source_target_pairs={{0,48},{16,0},{32,16},{48,32},{64,112},{80,64},{96,80},{112,96},{1... | collective-permute-start | bytes 2359304 | tf_op jit(solution)/shard_map/ppermute | solution.py:426
  81.9 0.1 copy.18
  82.0 14.3 %columns.2.refs_14_ = f32[96,128]{1,0:T(8,128)} custom-call(bf16[512,256]{1,0:T(8,128)(2,1)} %get-tuple-element.27.refs_0_, bf16[2,48,16,128]{3,2,1,0:T(8,128)(2,1)} %copy-done.2, bf16[2,48,16,128]{3,2,1,0:T(8,128)(2,1)} %copy-done.3, bf16[2,48,16,128]{3,2,1,0:T(8,128)(2,1)} %copy-done.7, bf16[2,48,16,128]{3,2,1,0:T(8,128)(2,1)} %copy-done.10, ...), custom_call_target="tpu_custom_call" | custom-call | flops 100000 | bytes 100000 | tf_op jit(solution)/shard_map/columns/pallas_call | solution.py:389
  96.4 9.6 %collective-permute-done.22.refs_7_ = bf16[2,96,16,128]{3,2,1,0:T(8,128)(2,1)S(1)} collective-permute-done((bf16[2,96,16,128]{3,2,1,0:T(8,128)(2,1)S(1)}, bf16[2,96,16,128]{3,2,1,0:T(8,128)(2,1)S(1)}, u32[]{:S(2)}, u32[]{:S(2)}) %collective-permute-start.22) | collective-permute-done | bytes 786464 | tf_op jit(solution)/shard_map/ppermute | solution.py:426
  106.0 2.5 %collective-permute-done.23.refs_8_ = bf16[2,96,16,128]{3,2,1,0:T(8,128)(2,1)} collective-permute-done((bf16[2,96,16,128]{3,2,1,0:T(8,128)(2,1)}, bf16[2,96,16,128]{3,2,1,0:T(8,128)(2,1)}, u32[]{:S(2)}, u32[]{:S(2)}) %collective-permute-start.23) | collective-permute-done | bytes 786464 | tf_op jit(solution)/shard_map/ppermute | solution.py:426
  108.5 21.0 %columns.3 = f32[16,8,256]{2,1,0:T(8,128)} custom-call(bf16[512,256]{1,0:T(8,128)(2,1)} %get-tuple-element.27.refs_0_, bf16[2,96,16,128]{3,2,1,0:T(8,128)(2,1)} %copy-done, bf16[2,96,16,128]{3,2,1,0:T(8,128)(2,1)} %copy-done.1, bf16[2,96,16,128]{3,2,1,0:T(8,128)(2,1)} %copy-done.4, bf16[2,96,16,128]{3,2,1,0:T(8,128)(2,1)} %collective-permute-done.18.refs_4_, ...), custom_call_target="tpu_custom_call" | custom-call | flops 100000 | bytes 100000 | tf_op jit(solution)/shard_map/columns/pallas_call | solution.py:389
  129.5 6.4 %all-to-all-start = ((f32[16,8,256]{2,1,0:T(8,128)}), f32[16,8,256]{2,1,0:T(8,128)S(1)}, u32[]{:S(2)}, u32[]{:S(2)}) async-start(f32[16,8,256]{2,1,0:T(8,128)} %columns.3), calls=%async_computation | async-start | bytes 262144 | tf_op jit(solution)/shard_map/all_to_all | solution.py:524
  135.9 0.6 gather_fusion
  136.4 8.3 %all-to-all-done = f32[16,8,256]{2,1,0:T(8,128)S(1)} async-done(((f32[16,8,256]{2,1,0:T(8,128)}), f32[16,8,256]{2,1,0:T(8,128)S(1)}, u32[]{:S(2)}, u32[]{:S(2)}) %all-to-all-start) | async-done | bytes 131104 | tf_op jit(solution)/shard_map/all_to_all | solution.py:524
  144.8 0.1 reshape.27
  145.0 0.1 slice.23
  145.2 0.6 fusion.1
  (71 shorter events, 0.7 us)
Async XLA Ops:
  2.3 13.8 %collective-permute-start = (bf16[48,16,128]{2,1,0:T(8,128)(2,1)}, bf16[48,16,128]{2,1,0:T(8,128)(2,1)S(1)}, u32[]{:S(2)}, u32[]{:S(2)}) collective-permute-start(bf16[48,16,128]{2,1,0:T(8,128)(2,1)} %get-tuple-element.29), channel_id=1, source_target_pairs={{0,64},{16,80},{32,96},{48,112},{64,128},{80,144},{96,160},{112,17... | collective-permute-start | bytes 589832 | tf_op jit(solution)/shard_map/ppermute | solution.py:426
  4.2 12.0 %collective-permute-start.9 = (f32[48,512]{1,0:T(8,128)}, f32[48,512]{1,0:T(8,128)S(1)}, u32[]{:S(2)}, u32[]{:S(2)}) collective-permute-start(f32[48,512]{1,0:T(8,128)} %get-tuple-element.33), channel_id=1, source_target_pairs={{0,1},{1,0},{2,3},{3,2},{4,5},{5,4},{6,7},{7,6},{8,9},{9,8},{10,11... | collective-permute-start | bytes 294920 | tf_op jit(solution)/shard_map/ppermute | solution.py:430
  4.2 11.9 %collective-permute-start.1 = (s32[1,256]{1,0:T(1,128)}, s32[1,256]{1,0:T(1,128)S(1)}, u32[]{:S(2)}, u32[]{:S(2)}) collective-permute-start(s32[1,256]{1,0:T(1,128)} %get-tuple-element.23), channel_id=1, source_target_pairs={{0,8},{1,9},{2,10},{3,11},{4,12},{5,13},{6,14},{7,15},{8,0},{9,1},... | collective-permute-start | bytes 3080 | tf_op jit(solution)/shard_map/ppermute | solution.py:430
  10.5 11.1 %collective-permute-start.3 = (bf16[48,16,128]{2,1,0:T(8,128)(2,1)}, bf16[48,16,128]{2,1,0:T(8,128)(2,1)S(1)}, u32[]{:S(2)}, u32[]{:S(2)}) collective-permute-start(bf16[48,16,128]{2,1,0:T(8,128)(2,1)} %get-tuple-element.29), channel_id=1, source_target_pairs={{0,192},{16,208},{32,224},{48,240},{64,0},{80,16},{96,32},{112,48}... | collective-permute-start | bytes 589832 | tf_op jit(solution)/shard_map/ppermute | solution.py:426
  16.0 8.6 %collective-permute-start.2 = (bf16[48,16,128]{2,1,0:T(8,128)(2,1)S(1)}, bf16[48,16,128]{2,1,0:T(8,128)(2,1)S(1)}, u32[]{:S(2)}, u32[]{:S(2)}) collective-permute-start(bf16[48,16,128]{2,1,0:T(8,128)(2,1)S(1)} %collective-permute-done), channel_id=1, source_target_pairs={{0,64},{16,80},{32,96},{48,112},{64,128},{80,144},{96,160},{112,17... | collective-permute-start | bytes 589832 | tf_op jit(solution)/shard_map/ppermute | solution.py:426
  17.0 15.4 %copy-start.6 = (f32[2,48,512]{2,1,0:T(8,128)}, f32[2,48,512]{2,1,0:T(8,128)S(1)}, u32[]{:S(2)}) copy-start(f32[2,48,512]{2,1,0:T(8,128)S(1)} %pad_maximum_fusion.4.refs_0_) | copy-start | bytes 589828
  17.1 10.7 %collective-permute-start.10 = (f32[2,48,512]{2,1,0:T(8,128)S(1)}, f32[2,48,512]{2,1,0:T(8,128)S(1)}, u32[]{:S(2)}, u32[]{:S(2)}) collective-permute-start(f32[2,48,512]{2,1,0:T(8,128)S(1)} %pad_maximum_fusion.4.refs_0_), channel_id=1, source_target_pairs={{0,2},{1,3},{2,4},{3,5},{4,6},{5,7},{6,0},{7,1},{8,10},{9,11},{10,... | collective-permute-start | bytes 589832 | tf_op jit(solution)/shard_map/ppermute | solution.py:430
  17.6 11.9 %collective-permute-start.11 = (f32[2,48,512]{2,1,0:T(8,128)S(1)}, f32[2,48,512]{2,1,0:T(8,128)S(1)}, u32[]{:S(2)}, u32[]{:S(2)}) collective-permute-start(f32[2,48,512]{2,1,0:T(8,128)S(1)} %pad_maximum_fusion.4.refs_0_), channel_id=1, source_target_pairs={{0,6},{1,7},{2,0},{3,1},{4,2},{5,3},{6,4},{7,5},{8,14},{9,15},{10,... | collective-permute-start | bytes 589832 | tf_op jit(solution)/shard_map/ppermute | solution.py:430
  19.2 10.4 %collective-permute-start.12 = (f32[2,48,512]{2,1,0:T(8,128)S(1)}, f32[2,48,512]{2,1,0:T(8,128)S(1)}, u32[]{:S(2)}, u32[]{:S(2)}) collective-permute-start(f32[2,48,512]{2,1,0:T(8,128)S(1)} %pad_maximum_fusion.4.refs_0_), channel_id=1, source_target_pairs={{0,4},{1,5},{2,6},{3,7},{4,0},{5,1},{6,2},{7,3},{8,12},{9,13},{10,... | collective-permute-start | bytes 589832 | tf_op jit(solution)/shard_map/ppermute | solution.py:430
  21.5 56.8 %copy-start.2 = (bf16[2,48,16,128]{3,2,1,0:T(8,128)(2,1)}, bf16[2,48,16,128]{3,2,1,0:T(8,128)(2,1)S(1)}, u32[]{:S(2)}) copy-start(bf16[2,48,16,128]{3,2,1,0:T(8,128)(2,1)S(1)} %pad_maximum_fusion.3.refs_1_) | copy-start | bytes 1179652
  21.6 13.7 %collective-permute-start.7 = (bf16[2,48,16,128]{3,2,1,0:T(8,128)(2,1)S(1)}, bf16[2,48,16,128]{3,2,1,0:T(8,128)(2,1)S(1)}, u32[]{:S(2)}, u32[]{:S(2)}) collective-permute-start(bf16[2,48,16,128]{3,2,1,0:T(8,128)(2,1)S(1)} %pad_maximum_fusion.3.refs_1_), channel_id=1, source_target_pairs={{0,16},{16,32},{32,48},{48,0},{64,80},{80,96},{96,112},{112,64},{1... | collective-permute-start | bytes 1179656 | tf_op jit(solution)/shard_map/ppermute | solution.py:426
  24.7 14.3 %collective-permute-start.8 = (bf16[2,48,16,128]{3,2,1,0:T(8,128)(2,1)S(1)}, bf16[2,48,16,128]{3,2,1,0:T(8,128)(2,1)S(1)}, u32[]{:S(2)}, u32[]{:S(2)}) collective-permute-start(bf16[2,48,16,128]{3,2,1,0:T(8,128)(2,1)S(1)} %pad_maximum_fusion.3.refs_1_), channel_id=1, source_target_pairs={{0,48},{16,0},{32,16},{48,32},{64,112},{80,64},{96,80},{112,96},{1... | collective-permute-start | bytes 1179656 | tf_op jit(solution)/shard_map/ppermute | solution.py:426
  27.7 50.6 %copy-start.3 = (bf16[2,48,16,128]{3,2,1,0:T(8,128)(2,1)}, bf16[2,48,16,128]{3,2,1,0:T(8,128)(2,1)S(1)}, u32[]{:S(2)}) copy-start(bf16[2,48,16,128]{3,2,1,0:T(8,128)(2,1)S(1)} %pad_maximum_fusion.2.refs_2_) | copy-start | bytes 1179652
  27.7 4.7 %copy-start.13 = (f32[2,48,512]{2,1,0:T(8,128)}, f32[2,48,512]{2,1,0:T(8,128)S(1)}, u32[]{:S(2)}) copy-start(f32[2,48,512]{2,1,0:T(8,128)S(1)} %collective-permute-done.10.refs_1_) | copy-start | bytes 589828
  27.8 16.0 %collective-permute-start.6 = (bf16[2,48,16,128]{3,2,1,0:T(8,128)(2,1)S(1)}, bf16[2,48,16,128]{3,2,1,0:T(8,128)(2,1)S(1)}, u32[]{:S(2)}, u32[]{:S(2)}) collective-permute-start(bf16[2,48,16,128]{3,2,1,0:T(8,128)(2,1)S(1)} %pad_maximum_fusion.2.refs_2_), channel_id=1, source_target_pairs={{0,48},{16,0},{32,16},{48,32},{64,112},{80,64},{96,80},{112,96},{1... | collective-permute-start | bytes 1179656 | tf_op jit(solution)/shard_map/ppermute | solution.py:426
  29.5 2.9 %copy-start.14 = (f32[2,48,512]{2,1,0:T(8,128)}, f32[2,48,512]{2,1,0:T(8,128)S(1)}, u32[]{:S(2)}) copy-start(f32[2,48,512]{2,1,0:T(8,128)S(1)} %collective-permute-done.11.refs_2_) | copy-start | bytes 589828
  29.5 13.1 %collective-permute-start.4 = (bf16[96,16,128]{2,1,0:T(8,128)(2,1)}, bf16[96,16,128]{2,1,0:T(8,128)(2,1)S(1)}, u32[]{:S(2)}, u32[]{:S(2)}) collective-permute-start(bf16[96,16,128]{2,1,0:T(8,128)(2,1)} %get-tuple-element.32), channel_id=1, source_target_pairs={{0,64},{16,80},{32,96},{48,112},{64,128},{80,144},{96,160},{112,17... | collective-permute-start | bytes 1179656 | tf_op jit(solution)/shard_map/ppermute | solution.py:426
  29.5 2.9 %copy-start.15 = (f32[2,48,512]{2,1,0:T(8,128)}, f32[2,48,512]{2,1,0:T(8,128)S(1)}, u32[]{:S(2)}) copy-start(f32[2,48,512]{2,1,0:T(8,128)S(1)} %collective-permute-done.12.refs_3_) | copy-start | bytes 589828
  29.5 14.2 %collective-permute-start.5 = (bf16[2,48,16,128]{3,2,1,0:T(8,128)(2,1)S(1)}, bf16[2,48,16,128]{3,2,1,0:T(8,128)(2,1)S(1)}, u32[]{:S(2)}, u32[]{:S(2)}) collective-permute-start(bf16[2,48,16,128]{3,2,1,0:T(8,128)(2,1)S(1)} %pad_maximum_fusion.2.refs_2_), channel_id=1, source_target_pairs={{0,16},{16,32},{32,48},{48,0},{64,80},{80,96},{96,112},{112,64},{1... | collective-permute-start | bytes 1179656 | tf_op jit(solution)/shard_map/ppermute | solution.py:426
  35.2 43.1 %copy-start.7 = (bf16[2,48,16,128]{3,2,1,0:T(8,128)(2,1)}, bf16[2,48,16,128]{3,2,1,0:T(8,128)(2,1)S(1)}, u32[]{:S(2)}) copy-start(bf16[2,48,16,128]{3,2,1,0:T(8,128)(2,1)S(1)} %collective-permute-done.7.refs_3_) | copy-start | bytes 1179652
  35.2 15.4 %collective-permute-start.14 = (bf16[96,16,128]{2,1,0:T(8,128)(2,1)}, bf16[96,16,128]{2,1,0:T(8,128)(2,1)S(1)}, u32[]{:S(2)}, u32[]{:S(2)}) collective-permute-start(bf16[96,16,128]{2,1,0:T(8,128)(2,1)} %get-tuple-element.32), channel_id=1, source_target_pairs={{0,192},{16,208},{32,224},{48,240},{64,0},{80,16},{96,32},{112,48}... | collective-permute-start | bytes 1179656 | tf_op jit(solution)/shard_map/ppermute | solution.py:426
  39.0 4.8 %copy-start.8 = (bf16[2,48,16,128]{3,2,1,0:T(8,128)(2,1)}, bf16[2,48,16,128]{3,2,1,0:T(8,128)(2,1)S(1)}, u32[]{:S(2)}) copy-start(bf16[2,48,16,128]{3,2,1,0:T(8,128)(2,1)S(1)} %collective-permute-done.8.refs_5_) | copy-start | bytes 1179652
  43.7 34.6 %copy-start.9 = (bf16[2,48,16,128]{3,2,1,0:T(8,128)(2,1)}, bf16[2,48,16,128]{3,2,1,0:T(8,128)(2,1)S(1)}, u32[]{:S(2)}) copy-start(bf16[2,48,16,128]{3,2,1,0:T(8,128)(2,1)S(1)} %collective-permute-done.6.refs_6_) | copy-start | bytes 1179652
  43.7 4.2 %copy-start.10 = (bf16[2,48,16,128]{3,2,1,0:T(8,128)(2,1)}, bf16[2,48,16,128]{3,2,1,0:T(8,128)(2,1)S(1)}, u32[]{:S(2)}) copy-start(bf16[2,48,16,128]{3,2,1,0:T(8,128)(2,1)S(1)} %collective-permute-done.5.refs_4_) | copy-start | bytes 1179652
  43.7 13.2 %collective-permute-start.13 = (bf16[96,16,128]{2,1,0:T(8,128)(2,1)S(1)}, bf16[96,16,128]{2,1,0:T(8,128)(2,1)S(1)}, u32[]{:S(2)}, u32[]{:S(2)}) collective-permute-start(bf16[96,16,128]{2,1,0:T(8,128)(2,1)S(1)} %collective-permute-done.4), channel_id=1, source_target_pairs={{0,64},{16,80},{32,96},{48,112},{64,128},{80,144},{96,160},{112,17... | collective-permute-start | bytes 1179656 | tf_op jit(solution)/shard_map/ppermute | solution.py:426
  44.3 13.7 %collective-permute-start.16 = (bf16[2,48,16,128]{3,2,1,0:T(8,128)(2,1)S(1)}, bf16[2,48,16,128]{3,2,1,0:T(8,128)(2,1)S(1)}, u32[]{:S(2)}, u32[]{:S(2)}) collective-permute-start(bf16[2,48,16,128]{3,2,1,0:T(8,128)(2,1)S(1)} %collective-permute-done.7.refs_3_), channel_id=1, source_target_pairs={{0,16},{16,32},{32,48},{48,0},{64,80},{80,96},{96,112},{112,64},{1... | collective-permute-start | bytes 1179656 | tf_op jit(solution)/shard_map/ppermute | solution.py:426
  45.3 12.7 %collective-permute-start.17 = (bf16[2,48,16,128]{3,2,1,0:T(8,128)(2,1)S(1)}, bf16[2,48,16,128]{3,2,1,0:T(8,128)(2,1)S(1)}, u32[]{:S(2)}, u32[]{:S(2)}) collective-permute-start(bf16[2,48,16,128]{3,2,1,0:T(8,128)(2,1)S(1)} %collective-permute-done.6.refs_6_), channel_id=1, source_target_pairs={{0,48},{16,0},{32,16},{48,32},{64,112},{80,64},{96,80},{112,96},{1... | collective-permute-start | bytes 1179656 | tf_op jit(solution)/shard_map/ppermute | solution.py:426
  49.0 29.4 %copy-start = (bf16[2,96,16,128]{3,2,1,0:T(8,128)(2,1)}, bf16[2,96,16,128]{3,2,1,0:T(8,128)(2,1)S(1)}, u32[]{:S(2)}) copy-start(bf16[2,96,16,128]{3,2,1,0:T(8,128)(2,1)S(1)} %pad_maximum_fusion.refs_1_) | copy-start | bytes 2359300
  49.0 29.4 %collective-permute-start.15 = (bf16[2,96,16,128]{3,2,1,0:T(8,128)(2,1)S(1)}, bf16[2,96,16,128]{3,2,1,0:T(8,128)(2,1)S(1)}, u32[]{:S(2)}, u32[]{:S(2)}) collective-permute-start(bf16[2,96,16,128]{3,2,1,0:T(8,128)(2,1)S(1)} %pad_maximum_fusion.refs_1_), channel_id=1, source_target_pairs={{0,16},{16,32},{32,48},{48,0},{64,80},{80,96},{96,112},{112,64},{1... | collective-permute-start | bytes 2359304 | tf_op jit(solution)/shard_map/ppermute | solution.py:426
  57.0 24.9 %copy-start.17 = (s32[512,12]{0,1:T(8,128)S(1)}, s32[512,12]{0,1:T(8,128)}, u32[]{:S(2)}) copy-start(s32[512,12]{0,1:T(8,128)} %param.22) | copy-start | bytes 73732
  57.1 39.3 %copy-start.1 = (bf16[2,96,16,128]{3,2,1,0:T(8,128)(2,1)}, bf16[2,96,16,128]{3,2,1,0:T(8,128)(2,1)S(1)}, u32[]{:S(2)}) copy-start(bf16[2,96,16,128]{3,2,1,0:T(8,128)(2,1)S(1)} %pad_maximum_fusion.1.refs_2_) | copy-start | bytes 2359300
  58.0 20.4 %copy-start.11 = (bf16[2,48,16,128]{3,2,1,0:T(8,128)(2,1)}, bf16[2,48,16,128]{3,2,1,0:T(8,128)(2,1)S(1)}, u32[]{:S(2)}) copy-start(bf16[2,48,16,128]{3,2,1,0:T(8,128)(2,1)S(1)} %collective-permute-done.16.refs_7_) | copy-start | bytes 1179652
  58.0 20.4 %copy-start.12 = (bf16[2,48,16,128]{3,2,1,0:T(8,128)(2,1)}, bf16[2,48,16,128]{3,2,1,0:T(8,128)(2,1)S(1)}, u32[]{:S(2)}) copy-start(bf16[2,48,16,128]{3,2,1,0:T(8,128)(2,1)S(1)} %collective-permute-done.17.refs_8_) | copy-start | bytes 1179652
  58.0 20.7 %collective-permute-start.20 = (bf16[2,96,16,128]{3,2,1,0:T(8,128)(2,1)S(1)}, bf16[2,96,16,128]{3,2,1,0:T(8,128)(2,1)}, u32[]{:S(2)}, u32[]{:S(2)}) collective-permute-start(bf16[2,96,16,128]{3,2,1,0:T(8,128)(2,1)S(1)} %pad_maximum_fusion.1.refs_2_), channel_id=1, source_target_pairs={{0,48},{16,0},{32,16},{48,32},{64,112},{80,64},{96,80},{112,96},{1... | collective-permute-start | bytes 2359304 | tf_op jit(solution)/shard_map/ppermute | solution.py:426
  60.9 17.5 %collective-permute-start.21 = (f32[1,48,256]{2,1,0:T(8,128)S(1)}, f32[1,48,256]{2,1,0:T(8,128)S(1)}, u32[]{:S(2)}, u32[]{:S(2)}) collective-permute-start(f32[1,48,256]{2,1,0:T(8,128)S(1)} %slice.27), channel_id=1, source_target_pairs={{0,8},{1,9},{2,10},{3,11},{4,12},{5,13},{6,14},{7,15},{8,0},{9,1},... | collective-permute-start | bytes 147464 | tf_op jit(solution)/shard_map/ppermute | solution.py:430
  62.4 34.0 %collective-permute-start.19 = (bf16[2,96,16,128]{3,2,1,0:T(8,128)(2,1)S(1)}, bf16[2,96,16,128]{3,2,1,0:T(8,128)(2,1)}, u32[]{:S(2)}, u32[]{:S(2)}) collective-permute-start(bf16[2,96,16,128]{3,2,1,0:T(8,128)(2,1)S(1)} %pad_maximum_fusion.refs_1_), channel_id=1, source_target_pairs={{0,48},{16,0},{32,16},{48,32},{64,112},{80,64},{96,80},{112,96},{1... | collective-permute-start | bytes 2359304 | tf_op jit(solution)/shard_map/ppermute | solution.py:426
  63.1 33.3 %collective-permute-start.18 = (bf16[2,96,16,128]{3,2,1,0:T(8,128)(2,1)S(1)}, bf16[2,96,16,128]{3,2,1,0:T(8,128)(2,1)}, u32[]{:S(2)}, u32[]{:S(2)}) collective-permute-start(bf16[2,96,16,128]{3,2,1,0:T(8,128)(2,1)S(1)} %pad_maximum_fusion.1.refs_2_), channel_id=1, source_target_pairs={{0,16},{16,32},{32,48},{48,0},{64,80},{80,96},{96,112},{112,64},{1... | collective-permute-start | bytes 2359304 | tf_op jit(solution)/shard_map/ppermute | solution.py:426
  78.4 0.6 copy-start.16
  78.4 30.0 %copy-start.4 = (bf16[2,96,16,128]{3,2,1,0:T(8,128)(2,1)}, bf16[2,96,16,128]{3,2,1,0:T(8,128)(2,1)S(1)}, u32[]{:S(2)}) copy-start(bf16[2,96,16,128]{3,2,1,0:T(8,128)(2,1)S(1)} %collective-permute-done.15.refs_3_) | copy-start | bytes 2359300
  78.5 27.5 %collective-permute-start.22 = (bf16[2,96,16,128]{3,2,1,0:T(8,128)(2,1)S(1)}, bf16[2,96,16,128]{3,2,1,0:T(8,128)(2,1)S(1)}, u32[]{:S(2)}, u32[]{:S(2)}) collective-permute-start(bf16[2,96,16,128]{3,2,1,0:T(8,128)(2,1)S(1)} %collective-permute-done.15.refs_3_), channel_id=1, source_target_pairs={{0,16},{16,32},{32,48},{48,0},{64,80},{80,96},{96,112},{112,64},{1... | collective-permute-start | bytes 2359304 | tf_op jit(solution)/shard_map/ppermute | solution.py:426
  79.0 29.4 %collective-permute-start.23 = (bf16[2,96,16,128]{3,2,1,0:T(8,128)(2,1)}, bf16[2,96,16,128]{3,2,1,0:T(8,128)(2,1)}, u32[]{:S(2)}, u32[]{:S(2)}) collective-permute-start(bf16[2,96,16,128]{3,2,1,0:T(8,128)(2,1)} %collective-permute-done.20.refs_6_), channel_id=1, source_target_pairs={{0,48},{16,0},{32,16},{48,32},{64,112},{80,64},{96,80},{112,96},{1... | collective-permute-start | bytes 2359304 | tf_op jit(solution)/shard_map/ppermute | solution.py:426
  96.3 39.5 %copy-start.20 = (s32[2]{0:T(128)S(1)}, s32[2]{0:T(128)}, u32[]{:S(2)}) copy-start(s32[2]{0:T(128)} %kbatch_ref.1) | copy-start | bytes 28
  96.3 48.8 %copy-start.19 = (f32[2,12]{1,0:T(2,128)S(1)}, f32[2,12]{1,0:T(2,128)}, u32[]{:S(2)}) copy-start(f32[2,12]{1,0:T(2,128)} %param.25) | copy-start | bytes 292
  96.3 48.8 %copy-start.18 = (f32[2,3,12]{2,0,1:T(2,128)S(1)}, f32[2,3,12]{2,0,1:T(2,128)}, u32[]{:S(2)}) copy-start(f32[2,3,12]{2,0,1:T(2,128)} %param.24) | copy-start | bytes 868
  106.0 2.5 %copy-start.5 = (bf16[2,96,16,128]{3,2,1,0:T(8,128)(2,1)}, bf16[2,96,16,128]{3,2,1,0:T(8,128)(2,1)S(1)}, u32[]{:S(2)}) copy-start(bf16[2,96,16,128]{3,2,1,0:T(8,128)(2,1)S(1)} %collective-permute-done.22.refs_7_) | copy-start | bytes 2359300
  129.5 15.3 %all-to-all-start = ((f32[16,8,256]{2,1,0:T(8,128)}), f32[16,8,256]{2,1,0:T(8,128)S(1)}, u32[]{:S(2)}, u32[]{:S(2)}) async-start(f32[16,8,256]{2,1,0:T(8,128)} %columns.3), calls=%async_computation | async-start | bytes 262144 | tf_op jit(solution)/shard_map/all_to_all | solution.py:524
